TPU v7x, 32 devices: a whole 2x2x4 slice. The times are simulated.
32 devices in a mesh: dp: 2 (over core), seq: 4 (over y, x), tensor: 4 (over z).
Axes of the slice: x: 2, y: 2, z: 4, core: 2. Of those that a mesh axis runs over, the one named last changes fastest.
Arguments:
- inputs: bfloat16 [2, 8192, 2304], P('dp', 'seq'), may hold values from -40 to 40
- positions: int32 [2, 8192], P('dp', 'seq'), may hold values from 0 to 7679, as said below
- query_weight: bfloat16 [2304, 2048], P(('dp', 'seq'), 'tensor'), may hold values from -0.21875 to 0.21875
- key_weight: bfloat16 [2304, 1024], P(('dp', 'seq'), 'tensor'), may hold values from -0.21875 to 0.21875
- value_weight: bfloat16 [2304, 1024], P(('dp', 'seq'), 'tensor'), may hold values from -0.125 to 0.125
- output_weight: bfloat16 [2304, 2048], P(('dp', 'seq'), 'tensor'), may hold values from -4 to 4
- gate_weight: bfloat16 [2304, 9216], P(('dp', 'seq'), 'tensor'), may hold values from -0.125 to 0.125
- up_weight: bfloat16 [2304, 9216], P(('dp', 'seq'), 'tensor'), may hold values from -0.125 to 0.125
- down_weight: bfloat16 [2304, 9216], P(('dp', 'seq'), 'tensor'), may hold values from -0.0625 to 0.0625
- pre_attention: bfloat16 [2304], P(('dp', 'seq')), may hold values from -0.59765625 to 0.59765625
- post_attention: bfloat16 [2304], P(('dp', 'seq')), may hold values from -0.59765625 to 0.59765625
- pre_feedforward: bfloat16 [2304], P(('dp', 'seq')), may hold values from -0.59765625 to 0.59765625
- post_feedforward: bfloat16 [2304], P(('dp', 'seq')), may hold values from -0.59765625 to 0.59765625
- cotangent: bfloat16 [2, 8192, 2304], P('dp', 'seq'), may hold values from -6 to 6
Outputs:
- layer_output: bfloat16 [2, 8192, 2304], P('dp', 'seq')
- input_gradient: float32 [2, 8192, 2304], P('dp', 'seq')
- query_gradient: float32 [2304, 2048], P(('dp', 'seq'), 'tensor')
- key_gradient: float32 [2304, 1024], P(('dp', 'seq'), 'tensor')
- value_gradient: float32 [2304, 1024], P(('dp', 'seq'), 'tensor')
- output_gradient: float32 [2304, 2048], P(('dp', 'seq'), 'tensor')
- gate_gradient: float32 [2304, 9216], P(('dp', 'seq'), 'tensor')
- up_gradient: float32 [2304, 9216], P(('dp', 'seq'), 'tensor')
- down_gradient: float32 [2304, 9216], P(('dp', 'seq'), 'tensor')
- pre_attention_gradient: float32 [2304], P(('dp', 'seq'))
- post_attention_gradient: float32 [2304], P(('dp', 'seq'))
- pre_feedforward_gradient: float32 [2304], P(('dp', 'seq'))
- post_feedforward_gradient: float32 [2304], P(('dp', 'seq'))
Inputs may be any that keep to these rules, and one draw needn't show every extreme that they name: `positions`: each row packs documents: a token's position is its index within its document, rising by one from token to token and starting again at 0 where a document begins. Every row holds one main document that begins within the row's first 2048 tokens (at token 0 in the first row) and ends at token 7679, with at most two documents before it and one document of 512 tokens after it.
All inputs are finite; a program needn't handle non-finite values.
Results may differ from a plain program's by a relative error of at most 0.018.
The roundings to bfloat16 on the way count: a program that leaves them out, or rounds other values in their place, can miss the bound.
Values may be sent and summed in bfloat16 or wider, within the bound.
No kernel may reach another device: no remote copies, remote signals or barrier semaphores. Data moves between devices by JAX's collectives and lax.ppermute only.
A program may use at most 448 MiB of HBM per device.

v0:
```python
import jax
import jax.numpy as jnp
from jax import lax
from jax.sharding import PartitionSpec as P

HD = 256
WINDOW = 4096
CAP = 50


EPS = 1e-06
THETA = 10000.0
OVER_ROWS = (((0,), (0,)), ((), ()))
OVER_COLUMNS = (((1,), (1,)), ((), ()))


def normalize(values, gain):
    factor = lax.rsqrt(jnp.mean(values * values, axis=-1, keepdims=True) + EPS)
    return values * factor * (1.0 + gain)


def gelu_tanh(values):
    return jax.nn.gelu(values, approximate=True)


def angles(places, width):
    half = width // 2
    frequency = jnp.power(THETA, -2.0 * jnp.arange(half, dtype=jnp.float32) / width)
    turned = places.astype(jnp.float32)[:, None] * frequency[None, :]
    return (jnp.cos(turned), jnp.sin(turned))


def rotate(values, cosine, sine):
    half = values.shape[-1] // 2
    first = values[..., :half]
    second = values[..., half:]
    cosine = cosine[:, None, :]
    sine = sine[:, None, :]
    return jnp.concatenate(
        [first * cosine - second * sine, second * cosine + first * sine], axis=-1
    )


def block_scores(query_block, window_keys, place_block, lead):
    scores = jnp.einsum(
        "qgrd,tgd->grqt", query_block, window_keys, preferred_element_type=jnp.float32
    ) * HD ** (-0.5)
    bent = CAP * jnp.tanh(scores / CAP)
    spacing = (
        lead
        + jnp.arange(query_block.shape[0], dtype=jnp.int32)[:, None]
        - jnp.arange(window_keys.shape[0], dtype=jnp.int32)[None, :]
    )
    allowed = (spacing >= 0) & (spacing <= place_block[:, None]) & (spacing < WINDOW)
    return (bent, jnp.where(allowed, bent, -1e30))


def per_device(
    inputs,
    positions,
    query_weight,
    key_weight,
    value_weight,
    output_weight,
    gate_weight,
    up_weight,
    down_weight,
    pre_attention,
    post_attention,
    pre_feedforward,
    post_feedforward,
    cotangent,
):
    gathered = (
        lax.all_gather(query_weight, ("dp", "seq"), axis=0, tiled=True),
        lax.all_gather(key_weight, ("dp", "seq"), axis=0, tiled=True),
        lax.all_gather(value_weight, ("dp", "seq"), axis=0, tiled=True),
        lax.all_gather(output_weight, ("dp", "seq"), axis=0, tiled=True),
        lax.all_gather(gate_weight, ("dp", "seq"), axis=0, tiled=True),
        lax.all_gather(up_weight, ("dp", "seq"), axis=0, tiled=True),
        lax.all_gather(down_weight, ("dp", "seq"), axis=0, tiled=True),
        lax.all_gather(pre_attention, ("dp", "seq"), axis=0, tiled=True),
        lax.all_gather(post_attention, ("dp", "seq"), axis=0, tiled=True),
        lax.all_gather(pre_feedforward, ("dp", "seq"), axis=0, tiled=True),
        lax.all_gather(post_feedforward, ("dp", "seq"), axis=0, tiled=True),
    )
    query_full, key_full, value_full, output_full, gate_full, up_full, down_full = gathered[:7]
    attend_gain = gathered[7].astype(jnp.float32)
    attend_post = gathered[8].astype(jnp.float32)
    forward_gain = gathered[9].astype(jnp.float32)
    forward_post = gathered[10].astype(jnp.float32)
    scale = HD ** (-0.5)
    hidden = inputs[0].astype(jnp.float32)
    places = positions[0]
    rows = hidden.shape[0]
    local_heads = query_full.shape[1] // HD
    local_groups = key_full.shape[1] // HD
    repeat = local_heads // local_groups
    width = local_groups * HD
    normed_one = normalize(hidden, attend_gain).astype(jnp.bfloat16)
    query_linear = jnp.dot(normed_one, query_full, preferred_element_type=jnp.float32)
    key_linear = jnp.dot(normed_one, key_full, preferred_element_type=jnp.float32)
    value_low = jnp.dot(normed_one, value_full, preferred_element_type=jnp.float32).astype(
        jnp.bfloat16
    )
    cosine, sine = angles(places, HD)
    query_low = rotate(query_linear.reshape(rows, local_heads, HD), cosine, sine).astype(
        jnp.bfloat16
    )
    key_low = (
        rotate(key_linear.reshape(rows, local_groups, HD), cosine, sine)
        .astype(jnp.bfloat16)
        .reshape(rows, width)
    )
    count = lax.axis_size("seq")
    index = lax.axis_index("seq")
    reach = min((WINDOW + rows - 2) // rows, count - 1)
    all_keys, all_values = (
        lax.all_gather(key_low, "seq", axis=0, tiled=True),
        lax.all_gather(value_low, "seq", axis=0, tiled=True),
    )
    padding = jnp.zeros((reach * rows, width), jnp.bfloat16)
    window_keys = lax.dynamic_slice_in_dim(
        jnp.concatenate([padding, all_keys], axis=0), index * rows, (reach + 1) * rows, 0
    )
    window_values = lax.dynamic_slice_in_dim(
        jnp.concatenate([padding, all_values], axis=0), index * rows, (reach + 1) * rows, 0
    )
    span = window_keys.shape[0]
    window_keys = window_keys.reshape(span, local_groups, HD)
    window_values = window_values.reshape(span, local_groups, HD)
    block = min(512, rows)
    blocks = rows // block
    query_blocks = query_low.reshape(blocks, block, local_groups, repeat, HD)
    place_blocks = places.reshape(blocks, block)
    leads = reach * rows + jnp.arange(blocks, dtype=jnp.int32) * block

    def forward_block(item):
        query_block, place_block, lead = item
        bent, capped = block_scores(query_block, window_keys, place_block, lead)
        highest = jnp.max(capped, axis=-1, keepdims=True)
        total = highest + jnp.log(jnp.sum(jnp.exp(capped - highest), axis=-1, keepdims=True))
        shares_low = jnp.exp(capped - total).astype(jnp.bfloat16)
        heads = jnp.einsum(
            "grqt,tgd->qgrd", shares_low, window_values, preferred_element_type=jnp.float32
        )
        return (heads.astype(jnp.bfloat16), total)

    head_blocks, totals = lax.map(forward_block, (query_blocks, place_blocks, leads))
    heads_low = head_blocks.reshape(rows, local_heads * HD)
    attention_part = lax.dot_general(
        heads_low, output_full, OVER_COLUMNS, preferred_element_type=jnp.float32
    )
    attention_out = lax.psum(attention_part, "tensor")
    middle = hidden + normalize(attention_out, attend_post)
    normed_two = normalize(middle, forward_gain).astype(jnp.bfloat16)
    gate_linear = jnp.dot(normed_two, gate_full, preferred_element_type=jnp.float32)
    up_linear = jnp.dot(normed_two, up_full, preferred_element_type=jnp.float32)
    activated, gelu_backward = jax.vjp(gelu_tanh, gate_linear)
    mixed = (activated * up_linear).astype(jnp.bfloat16)
    feedforward_part = lax.dot_general(
        mixed, down_full, OVER_COLUMNS, preferred_element_type=jnp.float32
    )
    feedforward_out = lax.psum(feedforward_part, "tensor")
    result = (middle + normalize(feedforward_out, forward_post)).astype(jnp.bfloat16)[None]
    query_back, key_back, value_back, output_back, gate_back, up_back, down_back = (
        lax.all_gather(query_weight, ("dp", "seq"), axis=0, tiled=True),
        lax.all_gather(key_weight, ("dp", "seq"), axis=0, tiled=True),
        lax.all_gather(value_weight, ("dp", "seq"), axis=0, tiled=True),
        lax.all_gather(output_weight, ("dp", "seq"), axis=0, tiled=True),
        lax.all_gather(gate_weight, ("dp", "seq"), axis=0, tiled=True),
        lax.all_gather(up_weight, ("dp", "seq"), axis=0, tiled=True),
        lax.all_gather(down_weight, ("dp", "seq"), axis=0, tiled=True),
    )
    upstream = cotangent[0].astype(jnp.float32)
    ignored, norm_four = jax.vjp(normalize, feedforward_out, forward_post)
    fed_gradient, forward_post_gradient = norm_four(upstream)
    fed_low = fed_gradient.astype(jnp.bfloat16)
    down_gradient = lax.dot_general(fed_low, mixed, OVER_ROWS, preferred_element_type=jnp.float32)
    mixed_gradient = jnp.dot(fed_low, down_back, preferred_element_type=jnp.float32)
    gate_low = gelu_backward(mixed_gradient * up_linear)[0].astype(jnp.bfloat16)
    up_low = (mixed_gradient * activated).astype(jnp.bfloat16)
    gate_gradient = lax.dot_general(
        normed_two, gate_low, OVER_ROWS, preferred_element_type=jnp.float32
    )
    up_gradient = lax.dot_general(normed_two, up_low, OVER_ROWS, preferred_element_type=jnp.float32)
    normed_two_part = lax.dot_general(
        gate_low, gate_back, OVER_COLUMNS, preferred_element_type=jnp.float32
    ) + lax.dot_general(up_low, up_back, OVER_COLUMNS, preferred_element_type=jnp.float32)
    normed_two_gradient = lax.psum(normed_two_part, "tensor")
    ignored, norm_three = jax.vjp(normalize, middle, forward_gain)
    middle_part, forward_gain_gradient = norm_three(normed_two_gradient)
    middle_gradient = upstream + middle_part
    ignored, norm_two = jax.vjp(normalize, attention_out, attend_post)
    attention_gradient, attend_post_gradient = norm_two(middle_gradient)
    attention_low = attention_gradient.astype(jnp.bfloat16)
    output_gradient = lax.dot_general(
        attention_low, heads_low, OVER_ROWS, preferred_element_type=jnp.float32
    )
    heads_gradient = jnp.dot(attention_low, output_back, preferred_element_type=jnp.float32).astype(
        jnp.bfloat16
    )
    heads_blocks = heads_gradient.reshape(blocks, block, local_groups, repeat, HD)

    def backward_block(carry, item):
        key_sum, value_sum = carry
        query_block, place_block, lead, total, grad_block = item
        bent, capped = block_scores(query_block, window_keys, place_block, lead)
        shares = jnp.exp(capped - total)
        share_gradient = jnp.einsum(
            "qgrd,tgd->grqt", grad_block, window_values, preferred_element_type=jnp.float32
        )
        inner = jnp.sum(shares * share_gradient, axis=-1, keepdims=True)
        slope = bent / CAP
        score_low = (shares * (share_gradient - inner) * (1.0 - slope * slope)).astype(jnp.bfloat16)
        query_part = (
            jnp.einsum("grqt,tgd->qgrd", score_low, window_keys, preferred_element_type=jnp.float32)
            * scale
        ).astype(jnp.bfloat16)
        key_sum = (
            key_sum
            + jnp.einsum(
                "grqt,qgrd->tgd", score_low, query_block, preferred_element_type=jnp.float32
            )
            * scale
        )
        value_sum = value_sum + jnp.einsum(
            "grqt,qgrd->tgd",
            shares.astype(jnp.bfloat16),
            grad_block,
            preferred_element_type=jnp.float32,
        )
        return ((key_sum, value_sum), query_part)

    empty = jnp.zeros((span, local_groups, HD), jnp.float32)
    window_sums, query_parts = lax.scan(
        backward_block, (empty, empty), (query_blocks, place_blocks, leads, totals, heads_blocks)
    )
    key_window = window_sums[0].reshape(span, width)
    value_window = window_sums[1].reshape(span, width)
    zeros_full = jnp.zeros(((reach + count) * rows, width), jnp.float32)
    key_spread = lax.dynamic_update_slice_in_dim(zeros_full, key_window, index * rows, 0)[
        reach * rows :
    ]
    value_spread = lax.dynamic_update_slice_in_dim(zeros_full, value_window, index * rows, 0)[
        reach * rows :
    ]
    key_total, value_total = (
        lax.psum_scatter(key_spread, "seq", scatter_dimension=0, tiled=True),
        lax.psum_scatter(value_spread, "seq", scatter_dimension=0, tiled=True),
    )
    key_rot_low = key_total.astype(jnp.bfloat16).astype(jnp.float32).reshape(rows, local_groups, HD)
    key_grad_low = rotate(key_rot_low, cosine, -sine).astype(jnp.bfloat16).reshape(rows, width)
    value_grad_low = value_total.astype(jnp.bfloat16)
    query_rot = query_parts.reshape(rows, local_heads, HD).astype(jnp.float32)
    query_grad_low = (
        rotate(query_rot, cosine, -sine).astype(jnp.bfloat16).reshape(rows, local_heads * HD)
    )
    query_gradient = lax.dot_general(
        normed_one, query_grad_low, OVER_ROWS, preferred_element_type=jnp.float32
    )
    key_gradient = lax.dot_general(
        normed_one, key_grad_low, OVER_ROWS, preferred_element_type=jnp.float32
    )
    value_gradient = lax.dot_general(
        normed_one, value_grad_low, OVER_ROWS, preferred_element_type=jnp.float32
    )
    normed_one_part = lax.dot_general(
        query_grad_low, query_back, OVER_COLUMNS, preferred_element_type=jnp.float32
    )
    normed_one_part = normed_one_part + lax.dot_general(
        key_grad_low, key_back, OVER_COLUMNS, preferred_element_type=jnp.float32
    )
    normed_one_part = normed_one_part + lax.dot_general(
        value_grad_low, value_back, OVER_COLUMNS, preferred_element_type=jnp.float32
    )
    normed_one_gradient = lax.psum(normed_one_part, "tensor")
    ignored, norm_one = jax.vjp(normalize, hidden, attend_gain)
    hidden_part, attend_gain_gradient = norm_one(normed_one_gradient)
    input_gradient = (middle_gradient + hidden_part)[None]
    (
        query_share,
        key_share,
        value_share,
        output_share,
        gate_share,
        up_share,
        down_share,
        attend_gain_share,
        attend_post_share,
        forward_gain_share,
        forward_post_share,
    ) = (
        lax.psum_scatter(query_gradient, ("dp", "seq"), scatter_dimension=0, tiled=True),
        lax.psum_scatter(key_gradient, ("dp", "seq"), scatter_dimension=0, tiled=True),
        lax.psum_scatter(value_gradient, ("dp", "seq"), scatter_dimension=0, tiled=True),
        lax.psum_scatter(output_gradient, ("dp", "seq"), scatter_dimension=0, tiled=True),
        lax.psum_scatter(gate_gradient, ("dp", "seq"), scatter_dimension=0, tiled=True),
        lax.psum_scatter(up_gradient, ("dp", "seq"), scatter_dimension=0, tiled=True),
        lax.psum_scatter(down_gradient, ("dp", "seq"), scatter_dimension=0, tiled=True),
        lax.psum_scatter(attend_gain_gradient, ("dp", "seq"), scatter_dimension=0, tiled=True),
        lax.psum_scatter(attend_post_gradient, ("dp", "seq"), scatter_dimension=0, tiled=True),
        lax.psum_scatter(forward_gain_gradient, ("dp", "seq"), scatter_dimension=0, tiled=True),
        lax.psum_scatter(forward_post_gradient, ("dp", "seq"), scatter_dimension=0, tiled=True),
    )
    return (
        result,
        input_gradient,
        query_share,
        key_share,
        value_share,
        output_share,
        gate_share,
        up_share,
        down_share,
        attend_gain_share,
        attend_post_share,
        forward_gain_share,
        forward_post_share,
    )


def solution(mesh):
    placed = (
        P("dp", "seq", None),
        P("dp", "seq"),
        P(("dp", "seq"), "tensor"),
        P(("dp", "seq"), "tensor"),
        P(("dp", "seq"), "tensor"),
        P(("dp", "seq"), "tensor"),
        P(("dp", "seq"), "tensor"),
        P(("dp", "seq"), "tensor"),
        P(("dp", "seq"), "tensor"),
        P(("dp", "seq")),
        P(("dp", "seq")),
        P(("dp", "seq")),
        P(("dp", "seq")),
        P("dp", "seq", None),
    )
    return jax.shard_map(
        per_device,
        mesh=mesh,
        in_specs=placed,
        out_specs=(
            P("dp", "seq", None),
            P("dp", "seq", None),
            P(("dp", "seq"), "tensor"),
            P(("dp", "seq"), "tensor"),
            P(("dp", "seq"), "tensor"),
            P(("dp", "seq"), "tensor"),
            P(("dp", "seq"), "tensor"),
            P(("dp", "seq"), "tensor"),
            P(("dp", "seq"), "tensor"),
            P(("dp", "seq")),
            P(("dp", "seq")),
            P(("dp", "seq")),
            P(("dp", "seq")),
        ),
        check_vma=False,
    )
```

profile of v0, /device:TPU:0, one launch (start us, length us, event | category | flops | bytes accessed | tf_op | source)
XLA Modules:
  0.0 4628.5 jit_solution(10113945416181204872)
XLA Ops:
  21.1 28.9 all-reduce.11
  108.8 40.0 all-gather.14.cloned.1.call-done
  155.4 48.4 %all-gather.18.cloned.1.call-done = bf16[8192,256]{1,0:T(8,128)(2,1)} async-done(((bf16[2048,256]{1,0:T(8,128)(2,1)}), bf16[8192,256]{1,0:T(8,128)(2,1)}) %all-gather.18.cloned.1.call-update) | async-done | bytes 4194320 | tf_op jit(solution)/shard_map/all_gather | solution.py:120
  207.3 189.8 %while.31 = (s32[]{:T(128)}, bf16[4,512,1,2,256]{4,3,1,0,2:T(2,128)(2,1)}, f32[4,1,2,512,1]{3,2,4,1,0:T(2,128)}, s32[4]{0:T(128)S(1)}, s32[4,512]{1,0:T(4,128)S(...) while((s32[]{:T(128)}, ...), condition=%wide.region_4.5_spmd, body=%wide.region_1.4_spmd.sunk | while | flops 6549667328 | bytes 96513648 | solution.py:149
  239.1 14.4 fusion.240
  286.5 14.4 fusion.240
  415.7 628.1 %all-reduce.17.cloned.1.call-done = f32[2048,2304]{1,0:T(8,128)} async-done(((f32[2048,2304]{1,0:T(8,128)}), f32[2048,2304]{1,0:T(8,128)}) %all-reduce.17.cloned.1.call-update) | async-done | bytes 18874384 | tf_op jit(solution)/shard_map/psum | solution.py:154
  1074.8 33.8 all-gather.22.cloned.1.call-done
  1108.6 30.3 fusion.173
  1138.9 35.6 all-gather.24.cloned.1.call-done
  1174.5 37.0 multiply_convert_fusion.1
  1211.5 28.7 all-gather.26.cloned.1.call-done
  1240.2 30.4 fusion.174
  1271.4 628.9 %all-reduce.19.cloned.1.call-done = f32[2048,2304]{1,0:T(8,128)} async-done(((f32[2048,2304]{1,0:T(8,128)}), f32[2048,2304]{1,0:T(8,128)}) %all-reduce.19.cloned.1.call-update) | async-done | bytes 18874384 | tf_op jit(solution)/shard_map/psum | solution.py:164
  1922.4 20.6 fusion.123
  1943.0 44.3 multiply_convert_fusion
  1987.3 30.6 fusion.175
  2017.9 31.0 convolution_add_fusion
  2049.1 628.4 %all-reduce.21.cloned.1.call-done = f32[2048,2304]{1,0:T(8,128)} async-done(((f32[2048,2304]{1,0:T(8,128)}), f32[2048,2304]{1,0:T(8,128)}) %all-reduce.21.cloned.1.call-update) | async-done | bytes 18874384 | tf_op jit(solution)/shard_map/psum | solution.py:190
  2691.9 30.5 multiply_reduce_fusion.1
  2748.2 407.3 %while.32 = (s32[]{:T(128)}, f32[6144,1,256]{0,2,1:T(8,128)}, f32[6144,1,256]{0,2,1:T(8,128)}, bf16[4,512,1,2,256]{4,1,3,2,0:T(8,128)(2,1)}, bf16[4,512,1,2,256]...) while((s32[]{:T(128)}, f32[6144,1,256]{0,2,1:T(8,128)}, ...), condition=%wide.region_16.17_spmd.clone, body=%wide.region_14.16_spmd.clone.sunk | while | flops 16265510912 | bytes 317234944 | solution.py:236
  2770.6 21.3 fusion.250
  2791.9 23.5 fusion.251
  2830.8 17.2 fusion.253
  2870.2 21.3 fusion.250
  2891.5 23.5 fusion.251
  2932.2 18.1 fusion.253
  2972.6 21.3 fusion.250
  2993.9 23.5 fusion.251
  3034.6 18.1 fusion.253
  3075.0 21.3 fusion.250
  3096.3 23.5 fusion.251
  3137.0 18.1 fusion.253
  3188.0 60.6 %reduce-scatter.10.cloned.1.call-done = f32[2048,256]{0,1:T(8,128)} async-done(((f32[8192,256]{0,1:T(8,128)}), f32[2048,256]{0,1:T(8,128)}) %reduce-scatter.10.cloned.1.call-update) | async-done | bytes 2097168 | tf_op jit(solution)/shard_map/reduce_scatter | solution.py:249
  3263.7 74.3 %reduce-scatter.12.cloned.1.call-done = f32[2048,256]{0,1:T(8,128)} async-done(((f32[8192,256]{0,1:T(8,128)}), f32[2048,256]{0,1:T(8,128)}) %reduce-scatter.12.cloned.1.call-update) | async-done | bytes 2097168 | tf_op jit(solution)/shard_map/reduce_scatter | solution.py:250
  3338.0 21.0 add_add_fusion.4
  3382.0 30.4 fusion.180
  3412.5 31.0 fusion.178
  3443.6 31.0 fusion.179
  3492.4 496.2 %all-reduce.23.cloned.1.call-done = f32[2048,2304]{1,0:T(8,128)} async-done(((f32[2048,2304]{1,0:T(8,128)}), f32[2048,2304]{1,0:T(8,128)}) %all-reduce.23.cloned.1.call-update) | async-done | bytes 18874384 | tf_op jit(solution)/shard_map/psum | solution.py:277
  4000.7 29.0 all-reduce.10
  4032.3 22.9 fusion.126
  4055.2 49.2 %reduce-scatter.14.cloned.1.call-done = f32[288,512]{1,0:T(8,128)} async-done(((f32[2304,512]{1,0:T(8,128)}), f32[288,512]{1,0:T(8,128)}) %reduce-scatter.14.cloned.1.call-update) | async-done | bytes 589840 | tf_op jit(solution)/shard_map/reduce_scatter | solution.py:294
  4104.3 141.2 %reduce-scatter.26.cloned.1.call-done = f32[288,2304]{1,0:T(8,128)} async-done(((f32[2304,2304]{1,0:T(8,128)}), f32[288,2304]{1,0:T(8,128)}) %reduce-scatter.26.cloned.1.call-update) | async-done | bytes 2654224 | tf_op jit(solution)/shard_map/reduce_scatter | solution.py:300
  4245.6 141.4 %reduce-scatter.22.cloned.1.call-done = f32[288,2304]{1,0:T(8,128)} async-done(((f32[2304,2304]{1,0:T(8,128)}), f32[288,2304]{1,0:T(8,128)}) %reduce-scatter.22.cloned.1.call-update) | async-done | bytes 2654224 | tf_op jit(solution)/shard_map/reduce_scatter | solution.py:298
  4387.0 141.2 %reduce-scatter.24.cloned.1.call-done = f32[288,2304]{1,0:T(8,128)} async-done(((f32[2304,2304]{1,0:T(8,128)}), f32[288,2304]{1,0:T(8,128)}) %reduce-scatter.24.cloned.1.call-update) | async-done | bytes 2654224 | tf_op jit(solution)/shard_map/reduce_scatter | solution.py:299
  4528.2 46.5 %reduce-scatter.16.cloned.1.call-done = f32[288,256]{1,0:T(8,128)} async-done(((f32[2304,256]{1,0:T(8,128)}), f32[288,256]{1,0:T(8,128)}) %reduce-scatter.16.cloned.1.call-update) | async-done | bytes 294928 | tf_op jit(solution)/shard_map/reduce_scatter | solution.py:295
  4574.7 46.8 %reduce-scatter.18.cloned.1.call-done = f32[288,256]{1,0:T(8,128)} async-done(((f32[2304,256]{1,0:T(8,128)}), f32[288,256]{1,0:T(8,128)}) %reduce-scatter.18.cloned.1.call-update) | async-done | bytes 294928 | tf_op jit(solution)/shard_map/reduce_scatter | solution.py:296
  (344 shorter events, 613.5 us)
Async XLA Ops:
  7.2 54.3 %all-gather.12.cloned.1.call-start = ((), (), s32[]{:S(2)}) async-start(), calls=%async_computation.10 | async-start | bytes 1327104 | tf_op jit(solution)/shard_map/all_gather | solution.py:76
  7.9 64.6 %all-gather.16.cloned.1.call-start = ((), (), s32[]{:S(2)}) async-start(), calls=%async_computation.12 | async-start | bytes 1327104 | tf_op jit(solution)/shard_map/all_gather | solution.py:77
  8.7 85.1 %all-gather.10.cloned.1.call-start = ((), (), s32[]{:S(2)}) async-start(), calls=%async_computation.9 | async-start | bytes 2654208 | tf_op jit(solution)/shard_map/all_gather | solution.py:75
  9.4 139.4 %all-gather.14.cloned.1.call-start = ((), (), s32[]{:S(2)}) async-start(), calls=%async_computation.11 | async-start | bytes 5242880 | tf_op jit(solution)/shard_map/all_gather | solution.py:119
  15.6 82.4 %copy-start.26 = (f32[2048]{0:T(1024)}, f32[2048]{0:T(1024)S(1)}, u32[]{:S(2)}) copy-start(f32[2048]{0:T(1024)S(1)} %fusion.163) | copy-start | bytes 24580
  50.1 30.8 copy-start.45
  52.0 28.9 copy-start.24
  52.0 46.0 copy-start.20
  72.4 131.4 %all-gather.18.cloned.1.call-start = ((), (), s32[]{:S(2)}) async-start(), calls=%async_computation.13 | async-start | bytes 5242880 | tf_op jit(solution)/shard_map/all_gather | solution.py:120
  80.1 321.5 %all-gather.20.cloned.1.call-start = ((), (), s32[]{:S(2)}) async-start(), calls=%async_computation.14 | async-start | bytes 2654208 | tf_op jit(solution)/shard_map/all_gather | solution.py:78
  80.7 963.1 %all-reduce.17.cloned.1.call-start = ((), (), s32[]{:S(2)}) async-start(), calls=%async_computation.15 | async-start | bytes 37748736 | tf_op jit(solution)/shard_map/psum | solution.py:154
  413.5 695.1 %all-gather.22.cloned.1.call-start = ((), (), s32[]{:S(2)}) async-start(), calls=%async_computation.16 | async-start | bytes 11943936 | tf_op jit(solution)/shard_map/all_gather | solution.py:79
  414.3 760.2 %all-gather.24.cloned.1.call-start = ((), (), s32[]{:S(2)}) async-start(), calls=%async_computation.17 | async-start | bytes 11943936 | tf_op jit(solution)/shard_map/all_gather | solution.py:80
  415.0 825.2 %all-gather.26.cloned.1.call-start = ((), (), s32[]{:S(2)}) async-start(), calls=%async_computation.18 | async-start | bytes 11943936 | tf_op jit(solution)/shard_map/all_gather | solution.py:81
  415.6 1484.6 %all-reduce.19.cloned.1.call-start = ((), (), s32[]{:S(2)}) async-start(), calls=%async_computation.19 | async-start | bytes 37748736 | tf_op jit(solution)/shard_map/psum | solution.py:164
  415.7 647.4 %copy-start.18 = (f32[2304]{0:T(1024)}, f32[2304]{0:T(1024)S(1)}, u32[]{:S(2)}) copy-start(f32[2304]{0:T(1024)S(1)} %convert_add_fusion.3) | copy-start | bytes 27652
  415.7 648.0 %copy-start.22 = (f32[2304]{0:T(1024)}, f32[2304]{0:T(1024)S(1)}, u32[]{:S(2)}) copy-start(f32[2304]{0:T(1024)S(1)} %convert_add_fusion.2) | copy-start | bytes 27652
  1270.7 1406.7 %all-reduce.21.cloned.1.call-start = ((), (), s32[]{:S(2)}) async-start(), calls=%async_computation.20 | async-start | bytes 37748736 | tf_op jit(solution)/shard_map/psum | solution.py:190
  2048.9 628.5 %copy-start.23 = (f32[2304]{0:T(1024)S(1)}, f32[2304]{0:T(1024)}, u32[]{:S(2)}) copy-start(f32[2304]{0:T(1024)} %copy-done.22) | copy-start | bytes 27652
  2048.9 628.5 %copy-start.31 = (f32[2048]{0:T(1024)S(1)}, f32[2048]{0:T(1024)}, u32[]{:S(2)}) copy-start(f32[2048]{0:T(1024)} %copy-done.30) | copy-start | bytes 24580
  2048.9 1199.7 %reduce-scatter.10.cloned.1.call-start = ((), (), s32[]{:S(2)}) async-start(), calls=%async_computation.21 | async-start | bytes 10485760 | tf_op jit(solution)/shard_map/reduce_scatter | solution.py:249
  2049.0 642.8 %copy-start.36 = (f32[2048]{0:T(1024)S(1)}, f32[2048]{0:T(1024)}, u32[]{:S(2)}) copy-start(f32[2048]{0:T(1024)} %copy-done.35) | copy-start | bytes 24580
  2049.0 642.8 %copy-start.19 = (f32[2304]{0:T(1024)S(1)}, f32[2304]{0:T(1024)}, u32[]{:S(2)}) copy-start(f32[2304]{0:T(1024)} %copy-done.18) | copy-start | bytes 27652
  2049.0 642.8 %copy-start.29 = (f32[2048]{0:T(1024)S(1)}, f32[2048]{0:T(1024)}, u32[]{:S(2)}) copy-start(f32[2048]{0:T(1024)} %copy-done.28) | copy-start | bytes 24580
  2691.8 30.6 slice-start
  2691.8 30.5 copy-start.34
  2691.8 30.5 slice-start.1
  2691.8 30.5 slice-start.2
  2691.9 31.7 slice-start.3
  2691.9 32.3 slice-start.4
  2972.6 21.3 copy-start.5
  3163.1 174.9 %reduce-scatter.12.cloned.1.call-start = ((), (), s32[]{:S(2)}) async-start(), calls=%async_computation.22 | async-start | bytes 10485760 | tf_op jit(solution)/shard_map/reduce_scatter | solution.py:250
  3170.8 817.8 %all-reduce.23.cloned.1.call-start = ((), (), s32[]{:S(2)}) async-start(), calls=%async_computation.23 | async-start | bytes 37748736 | tf_op jit(solution)/shard_map/psum | solution.py:277
  3176.4 73.9 %copy-start.25 = (f32[1,2048]{1,0:T(1,128)S(1)}, f32[1,2048]{1,0:T(1,128)}, u32[]{:S(2)}) copy-start(f32[1,2048]{1,0:T(1,128)} %copy-done.24) | copy-start | bytes 24580
  3176.4 74.0 %copy-start.46 = (f32[128]{0:T(128)S(1)}, f32[128]{0:T(128)}, u32[]{:S(2)}) copy-start(f32[128]{0:T(128)} %copy-done.45) | copy-start | bytes 1540
  3176.4 79.2 %copy-start.16 = (bf16[2304,256]{1,0:T(8,128)(2,1)S(1)}, bf16[2304,256]{1,0:T(8,128)(2,1)}, u32[]{:S(2)}) copy-start(bf16[2304,256]{1,0:T(8,128)(2,1)} %all-gather.12.cloned.1.call-done) | copy-start | bytes 3538948
  3254.6 83.3 %copy-start.17 = (bf16[2304,256]{1,0:T(8,128)(2,1)S(1)}, bf16[2304,256]{1,0:T(8,128)(2,1)}, u32[]{:S(2)}) copy-start(bf16[2304,256]{1,0:T(8,128)(2,1)} %all-gather.16.cloned.1.call-done) | copy-start | bytes 3538948
  3359.1 696.1 %reduce-scatter.20.cloned.1.call-start = ((), (), s32[]{:S(2)}) async-start(), calls=%async_computation.27 | async-start | bytes 5308416 | tf_op jit(solution)/shard_map/reduce_scatter | solution.py:297
  3371.1 733.2 %reduce-scatter.14.cloned.1.call-start = ((), (), s32[]{:S(2)}) async-start(), calls=%async_computation.24 | async-start | bytes 5308416 | tf_op jit(solution)/shard_map/reduce_scatter | solution.py:294
  3382.0 863.6 %reduce-scatter.26.cloned.1.call-start = ((), (), s32[]{:S(2)}) async-start(), calls=%async_computation.30 | async-start | bytes 23887872 | tf_op jit(solution)/shard_map/reduce_scatter | solution.py:300
  3412.5 974.5 %reduce-scatter.22.cloned.1.call-start = ((), (), s32[]{:S(2)}) async-start(), calls=%async_computation.28 | async-start | bytes 23887872 | tf_op jit(solution)/shard_map/reduce_scatter | solution.py:298
  3443.5 1084.7 %reduce-scatter.24.cloned.1.call-start = ((), (), s32[]{:S(2)}) async-start(), calls=%async_computation.29 | async-start | bytes 23887872 | tf_op jit(solution)/shard_map/reduce_scatter | solution.py:299
  3474.6 1100.1 %reduce-scatter.16.cloned.1.call-start = ((), (), s32[]{:S(2)}) async-start(), calls=%async_computation.25 | async-start | bytes 2654208 | tf_op jit(solution)/shard_map/reduce_scatter | solution.py:295
  3483.6 1137.9 %reduce-scatter.18.cloned.1.call-start = ((), (), s32[]{:S(2)}) async-start(), calls=%async_computation.26 | async-start | bytes 2654208 | tf_op jit(solution)/shard_map/reduce_scatter | solution.py:296
  3492.4 508.3 %copy-start.39 = (f32[2304]{0:T(1024)S(1)}, f32[2304]{0:T(1024)}, u32[]{:S(2)}) copy-start(f32[2304]{0:T(1024)} %get-tuple-element.333) | copy-start | bytes 27652
  3492.4 508.3 %copy-start.40 = (f32[2304]{0:T(1024)S(1)}, f32[2304]{0:T(1024)}, u32[]{:S(2)}) copy-start(f32[2304]{0:T(1024)} %get-tuple-element.329) | copy-start | bytes 27652
  3492.4 508.3 %copy-start.41 = (f32[2304]{0:T(1024)S(1)}, f32[2304]{0:T(1024)}, u32[]{:S(2)}) copy-start(f32[2304]{0:T(1024)} %get-tuple-element.331) | copy-start | bytes 27652
  3492.4 539.9 %copy-start.38 = (f32[2048]{0:T(1024)S(1)}, f32[2048]{0:T(1024)}, u32[]{:S(2)}) copy-start(f32[2048]{0:T(1024)} %copy-done.37) | copy-start | bytes 24580
  (45 other events, 432.5 us)
Sparse Core Ops, SparseCore 0:
  9.9 26.8 all-gather.11
  38.7 24.1 all-gather.15
  64.7 28.9 all-gather.9
  96.0 52.7 all-gather.13
  151.0 52.6 all-gather.17
  205.5 28.9 all-gather.19
  413.7 630.0 all-reduce.16
  1045.8 62.7 all-gather.21
  1110.6 63.7 all-gather.23
  1176.4 63.7 all-gather.25
  1270.8 629.3 all-reduce.18
  2049.1 628.3 all-reduce.20
  3163.2 85.3 reduce-scatter.9
  3251.5 86.4 reduce-scatter.11
  3359.2 629.3 all-reduce.22
  3992.5 53.6 reduce-scatter.19
  4050.4 53.8 reduce-scatter.13
  4108.4 137.1 reduce-scatter.25
  4249.8 137.1 reduce-scatter.21
  4391.0 137.1 reduce-scatter.23
  4532.2 42.4 reduce-scatter.15
  4579.0 42.4 reduce-scatter.17
where the time goes:
time: 4640 us; the launch traced here: 4630 us
  waiting for transfers between devices  3280 us (71%)
  matrix products  803 us (17%)
  other arithmetic  381 us (8%)
  local copies, waits for them, and re-layouts  86.2 us (2%)
  blocking collectives  57.9 us (1%)
    psum x1, waiting for transfers between devices, per_device(): feedforward_out = lax.psum(feedforward_part, 'tensor')  629 us
    psum x1, waiting for transfers between devices, per_device(): normed_two_gradient = lax.psum(normed_two_part, 'tensor')  628 us
    psum x1, waiting for transfers between devices, per_device(): attention_out = lax.psum(attention_part, 'tensor')  628 us
    psum x1, waiting for transfers between devices, per_device(): normed_one_gradient = lax.psum(normed_one_part, 'tensor')  496 us
    reduce_scatter x1, waiting for transfers between devices, per_device(): lax.psum_scatter(gate_gradient, ('dp', 'seq'), scatter_dimension=0, tiled...  141 us
    reduce_scatter x1, waiting for transfers between devices, per_device(): lax.psum_scatter(down_gradient, ('dp', 'seq'), scatter_dimension=0, tiled...  141 us
    reduce_scatter x1, waiting for transfers between devices, per_device(): lax.psum_scatter(up_gradient, ('dp', 'seq'), scatter_dimension=0, tiled=T...  141 us
    dot_general x8, matrix products, block_scores(): jnp.einsum('qgrd,tgd->grqt', query_block, window_keys, preferred_element_...  106 us
  transfers between devices with their start and end apart: 22, of which 18 were waited for; matrix products, arithmetic and copies ran while one was open for 12% of the time, Pallas kernels for 0%

commit v1 on v0

v1 whole, which is shorter than its diff:
```python
import functools

import jax
import jax.numpy as jnp
from jax import lax
from jax.experimental import pallas as pl
from jax.experimental.pallas import tpu as pltpu
from jax.sharding import PartitionSpec as P

HD = 256
WINDOW = 4096
CAP = 50
EPS = 1e-06
KEYS = 512
LOG2E = 1.4426950408889634
BEND = HD ** (-0.5) / CAP
RAISE = CAP * LOG2E
GELU = 0.7978845608028654
NT = (((1,), (1,)), ((), ()))
TN = (((0,), (0,)), ((), ()))
SMALL = pl.CostEstimate(flops=1, bytes_accessed=1, transcendentals=0)


def rotate(values, cosine, sine):
    half = HD // 2
    first, second = values[:, :half], values[:, half:]
    return jnp.concatenate([first * cosine - second * sine, second * cosine + first * sine], axis=1)


def stack_heads(block):
    return jnp.concatenate([block[:, :HD], block[:, HD:]], axis=0)


def load_pieces(pieces, window_ref, sems):
    rows = pieces[0].shape[0]
    copies = [
        pltpu.make_async_copy(piece, window_ref.at[pl.ds(i * rows, rows)], sems.at[i]) for i, piece in enumerate(pieces)
    ]
    for copy in copies:
        copy.start()
    for copy in copies:
        copy.wait()


def attend_kernel(first, number, bounds_ref, query_ref, low_ref, *rest):
    pieces, (heads_ref, stat_ref, acc_ref, sum_ref, window_ref, sems) = rest[:number], rest[number:]
    step = pl.program_id(0)

    @pl.when(step == 0)
    def _():
        load_pieces(pieces, window_ref, sems)

    chunk = query_ref.shape[0]
    base = (first + step) * chunk
    query = stack_heads(query_ref[...])
    acc_ref[...] = jnp.zeros_like(acc_ref)
    sum_ref[...] = jnp.zeros_like(sum_ref)

    def add_block(offset, size, masked, causal):
        rows = pl.ds(pl.multiple_of(base + offset, 256), size)
        keys = window_ref[rows, :HD]
        values = window_ref[rows, HD:]
        scores = lax.dot_general(query, keys, NT, preferred_element_type=jnp.float32)
        raised = jnp.exp2(jnp.tanh(scores * BEND) * RAISE)
        if masked:
            column = offset + lax.broadcasted_iota(jnp.int32, (chunk, size), 1)
            keep = column >= jnp.concatenate([low_ref[...]] * (size // 128), axis=1)
            if causal:
                keep &= column <= WINDOW + lax.broadcasted_iota(jnp.int32, (chunk, size), 0)
            raised = jnp.where(jnp.concatenate([keep, keep], axis=0), raised, 0.0)
        part = raised[:, :128]
        for lane in range(128, size, 128):
            part = part + raised[:, lane : lane + 128]
        sum_ref[...] += part
        acc_ref[...] += jnp.dot(raised.astype(jnp.bfloat16), values, preferred_element_type=jnp.float32)

    def masked_step(block, carry):
        add_block(block * KEYS, KEYS, True, False)
        return carry

    def full_step(block, carry):
        add_block(block * KEYS, KEYS, False, False)
        return carry

    blocks = WINDOW // KEYS
    lax.fori_loop(bounds_ref[first + step, 0], bounds_ref[first + step, 1], masked_step, 0)
    lax.fori_loop(bounds_ref[first + step, 1], blocks, full_step, 0)
    add_block(WINDOW, chunk, True, True)
    total = jnp.sum(sum_ref[...], axis=1, keepdims=True)
    heads = (acc_ref[...] / total).astype(jnp.bfloat16)
    heads_ref[:, :HD] = heads[:chunk]
    heads_ref[:, HD:] = heads[chunk:]
    stat_ref[...] = jnp.broadcast_to(jnp.log2(total), stat_ref.shape)


def attend(query, pieces, low, bounds, first, count, chunk):
    rows = count * chunk
    span = len(pieces) * pieces[0].shape[0]
    return pl.pallas_call(
        functools.partial(attend_kernel, first, len(pieces)),
        out_shape=(
            jax.ShapeDtypeStruct((rows, 2 * HD), jnp.bfloat16),
            jax.ShapeDtypeStruct((2 * rows, 128), jnp.float32),
        ),
        grid_spec=pltpu.PrefetchScalarGridSpec(
            num_scalar_prefetch=1,
            grid=(count,),
            in_specs=[
                pl.BlockSpec((chunk, 2 * HD), lambda g, b: (first + g, 0)),
                pl.BlockSpec((chunk, 128), lambda g, b: (first + g, 0)),
            ]
            + [pl.BlockSpec(memory_space=pl.ANY)] * len(pieces),
            out_specs=[
                pl.BlockSpec((chunk, 2 * HD), lambda g, b: (g, 0)),
                pl.BlockSpec((2 * chunk, 128), lambda g, b: (g, 0)),
            ],
            scratch_shapes=[
                pltpu.VMEM((2 * chunk, HD), jnp.float32),
                pltpu.VMEM((2 * chunk, 128), jnp.float32),
                pltpu.VMEM((span, 2 * HD), jnp.bfloat16),
                pltpu.SemaphoreType.DMA((len(pieces),)),
            ],
        ),
        compiler_params=pltpu.CompilerParams(vmem_limit_bytes=48 * 2**20),
        cost_estimate=SMALL,
        name="attend",
    )(bounds, query, low, *pieces)


def attend_back_kernel(
    first, number, carried, sent, bounds_ref, query_ref, grad_ref, heads_ref, stat_ref, low_ref, cosine_ref, sine_ref, *rest
):
    pieces, rest = rest[:number], rest[number:]
    if carried:
        before_ref, *rest = rest
    dquery_ref, *afters, sum_ref, acc_ref, window_ref, sem, sems = rest
    step = pl.program_id(0)
    chunk = query_ref.shape[0]
    base = (first + step) * chunk

    @pl.when(step == 0)
    def _():
        if carried:
            copy = pltpu.make_async_copy(before_ref, sum_ref, sem)
            copy.start()
        else:
            sum_ref[...] = jnp.zeros_like(sum_ref)
        load_pieces(pieces, window_ref, sems)
        if carried:
            copy.wait()

    query = stack_heads(query_ref[...])
    grad = stack_heads(grad_ref[...])
    heads = stack_heads(heads_ref[...])
    inner = jnp.sum(grad.astype(jnp.float32) * heads.astype(jnp.float32), axis=1, keepdims=True)
    inner = jnp.broadcast_to(inner, (2 * chunk, 128)).T[:1]
    stat = stat_ref[...].T[:1]
    low = low_ref[...]
    low = jnp.concatenate([low, low], axis=1)
    acc_ref[...] = jnp.zeros_like(acc_ref)

    def add_block(offset, size, masked, causal):
        place = pl.multiple_of(base + offset, 256)
        rows = pl.ds(place, size)
        keys = window_ref[rows, :HD]
        values = window_ref[rows, HD:]
        scores = lax.dot_general(keys, query, NT, preferred_element_type=jnp.float32)
        slope = jnp.tanh(scores * BEND)
        shares = jnp.exp2(slope * RAISE - stat)
        if masked:
            row = offset + lax.broadcasted_iota(jnp.int32, (size, 2 * chunk), 0)
            keep = row >= low
            if causal:
                column = lax.broadcasted_iota(jnp.int32, (size, chunk), 1)
                keep &= row <= WINDOW + jnp.concatenate([column, column], axis=1)
            shares = jnp.where(keep, shares, 0.0)
        share_grad = lax.dot_general(values, grad, NT, preferred_element_type=jnp.float32)
        score_low = (shares * (share_grad - inner) * (1.0 - slope * slope)).astype(jnp.bfloat16)
        sum_ref[rows, HD:] += jnp.dot(shares.astype(jnp.bfloat16), grad, preferred_element_type=jnp.float32)
        sum_ref[rows, :HD] += jnp.dot(score_low, query, preferred_element_type=jnp.float32)
        acc_ref[...] += lax.dot_general(keys, score_low, TN, preferred_element_type=jnp.float32)

    def masked_step(block, carry):
        add_block(block * KEYS, KEYS, True, False)
        return carry

    def full_step(block, carry):
        add_block(block * KEYS, KEYS, False, False)
        return carry

    blocks = WINDOW // KEYS
    lax.fori_loop(bounds_ref[first + step, 0], bounds_ref[first + step, 1], masked_step, 0)
    lax.fori_loop(bounds_ref[first + step, 1], blocks, full_step, 0)
    add_block(WINDOW, chunk, True, True)
    dquery = (acc_ref[...].T * HD ** (-0.5)).astype(jnp.bfloat16).astype(jnp.float32)
    for head in range(2):
        turned = rotate(dquery[head * chunk : (head + 1) * chunk], cosine_ref[...], -sine_ref[...])
        dquery_ref[:, head * HD : (head + 1) * HD] = turned.astype(jnp.bfloat16)

    @pl.when(step == pl.num_programs(0) - 1)
    def _():
        done = 0
        for out in afters[:-1]:
            out[...] = sum_ref[done : done + out.shape[0], :].astype(jnp.bfloat16)
            done += out.shape[0]
        copy = pltpu.make_async_copy(sum_ref.at[pl.ds(done, sum_ref.shape[0] - done)], afters[-1], sem)
        copy.start()
        copy.wait()


def attend_back(query, grad, heads, stat, pieces, low_row, cosine, sine, bounds, before, first, count, chunk,
                sent):
    rows = count * chunk
    span = len(pieces) * pieces[0].shape[0]
    carried = before is not None
    extra = [before] if carried else []
    return pl.pallas_call(
        functools.partial(attend_back_kernel, first, len(pieces), carried, sent),
        out_shape=(
            jax.ShapeDtypeStruct((rows, 2 * HD), jnp.bfloat16),
            *(jax.ShapeDtypeStruct((size, 2 * HD), jnp.bfloat16) for size in sent),
            jax.ShapeDtypeStruct((span - sum(sent), 2 * HD), jnp.float32),
        ),
        grid_spec=pltpu.PrefetchScalarGridSpec(
            num_scalar_prefetch=1,
            grid=(count,),
            in_specs=[
                pl.BlockSpec((chunk, 2 * HD), lambda g, b: (first + g, 0)),
                pl.BlockSpec((chunk, 2 * HD), lambda g, b: (g, 0)),
                pl.BlockSpec((chunk, 2 * HD), lambda g, b: (g, 0)),
                pl.BlockSpec((2 * chunk, 128), lambda g, b: (g, 0)),
                pl.BlockSpec((1, chunk), lambda g, b: (0, first + g)),
                pl.BlockSpec((chunk, HD // 2), lambda g, b: (first + g, 0)),
                pl.BlockSpec((chunk, HD // 2), lambda g, b: (first + g, 0)),
            ]
            + [pl.BlockSpec(memory_space=pl.ANY)] * (len(pieces) + len(extra)),
            out_specs=[
                pl.BlockSpec((chunk, 2 * HD), lambda g, b: (g, 0)),
                *(pl.BlockSpec((size, 2 * HD), lambda g, b: (0, 0)) for size in sent),
                pl.BlockSpec(memory_space=pl.ANY),
            ],
            scratch_shapes=[
                pltpu.VMEM((span, 2 * HD), jnp.float32),
                pltpu.VMEM((HD, 2 * chunk), jnp.float32),
                pltpu.VMEM((span, 2 * HD), jnp.bfloat16),
                pltpu.SemaphoreType.DMA,
                pltpu.SemaphoreType.DMA((len(pieces),)),
            ],
        ),
        compiler_params=pltpu.CompilerParams(vmem_limit_bytes=60 * 2**20),
        cost_estimate=SMALL,
        name="attend_back",
    )(bounds, query, grad, heads, stat, low_row, cosine, sine, *pieces, *extra)


def limits(places, chunk):
    count = places.shape[0] // chunk
    low = WINDOW + jnp.arange(chunk, dtype=jnp.int32)[None, :] - jnp.minimum(places.reshape(count, chunk), WINDOW - 1)
    blocks = WINDOW // KEYS
    begin = jnp.minimum(jnp.min(low, axis=1) // KEYS, blocks)
    full = jnp.minimum((jnp.max(low, axis=1) + KEYS - 1) // KEYS, blocks)
    return low.reshape(-1), jnp.stack([begin, full], axis=1)


def scaled(values):
    factor = lax.rsqrt(jnp.mean(values * values, axis=-1, keepdims=True) + EPS)
    return factor, values * factor


def project_group_kernel(hidden_ref, gain_ref, weight_ref, cosine_ref, sine_ref, normed_ref, own_ref, factor_ref):
    factor, normed = scaled(hidden_ref[...].astype(jnp.float32))
    factor_ref[...] = jnp.broadcast_to(factor, factor_ref.shape)
    normed = (normed * gain_ref[...]).astype(jnp.bfloat16)
    normed_ref[...] = normed
    linear = jnp.dot(normed, weight_ref[...], preferred_element_type=jnp.float32)
    own_ref[:, :HD] = rotate(linear[:, :HD], cosine_ref[...], sine_ref[...]).astype(jnp.bfloat16)
    own_ref[:, HD:] = linear[:, HD:].astype(jnp.bfloat16)


def project_group(hidden, gain, weight, cosine, sine):
    rows, features = hidden.shape
    tile = min(256, rows)
    return pl.pallas_call(
        project_group_kernel,
        out_shape=(
            jax.ShapeDtypeStruct((rows, features), jnp.bfloat16),
            jax.ShapeDtypeStruct((rows, 2 * HD), jnp.bfloat16),
            jax.ShapeDtypeStruct((rows, 128), jnp.float32),
        ),
        grid=(rows // tile,),
        in_specs=[
            pl.BlockSpec((tile, features), lambda g: (g, 0)),
            pl.BlockSpec((1, features), lambda g: (0, 0)),
            pl.BlockSpec((features, 2 * HD), lambda g: (0, 0), pipeline_mode=pl.Buffered(1)),
            pl.BlockSpec((tile, HD // 2), lambda g: (g, 0)),
            pl.BlockSpec((tile, HD // 2), lambda g: (g, 0)),
        ],
        out_specs=[
            pl.BlockSpec((tile, features), lambda g: (g, 0)),
            pl.BlockSpec((tile, 2 * HD), lambda g: (g, 0)),
            pl.BlockSpec((tile, 128), lambda g: (g, 0)),
        ],
        compiler_params=pltpu.CompilerParams(vmem_limit_bytes=32 * 2**20),
        cost_estimate=SMALL,
        name="project_group",
    )(hidden, gain, weight, cosine, sine)


def project_heads_kernel(normed_ref, weight_ref, cosine_ref, sine_ref, query_ref):
    linear = jnp.dot(normed_ref[...], weight_ref[...], preferred_element_type=jnp.float32)
    for head in range(0, 2 * HD, HD):
        turned = rotate(linear[:, head : head + HD], cosine_ref[...], sine_ref[...])
        query_ref[:, head : head + HD] = turned.astype(jnp.bfloat16)


def project_heads(normed, weight, cosine, sine):
    rows, features = normed.shape
    tile = min(256, rows)
    return pl.pallas_call(
        project_heads_kernel,
        out_shape=jax.ShapeDtypeStruct((rows, 2 * HD), jnp.bfloat16),
        grid=(rows // tile,),
        in_specs=[
            pl.BlockSpec((tile, features), lambda g: (g, 0)),
            pl.BlockSpec((features, 2 * HD), lambda g: (0, 0), pipeline_mode=pl.Buffered(1)),
            pl.BlockSpec((tile, HD // 2), lambda g: (g, 0)),
            pl.BlockSpec((tile, HD // 2), lambda g: (g, 0)),
        ],
        out_specs=pl.BlockSpec((tile, 2 * HD), lambda g: (g, 0)),
        compiler_params=pltpu.CompilerParams(vmem_limit_bytes=32 * 2**20),
        cost_estimate=SMALL,
        name="project_heads",
    )(normed, weight, cosine, sine)


def finish_group_kernel(cosine_ref, sine_ref, own_ref, *rest):
    *arrived, low_ref = rest
    total = own_ref[...]
    for block in arrived:
        total = total + block[...].astype(jnp.float32)
    key_rot = (total[:, :HD] * HD ** (-0.5)).astype(jnp.bfloat16).astype(jnp.float32)
    low_ref[:, :HD] = rotate(key_rot, cosine_ref[...], -sine_ref[...]).astype(jnp.bfloat16)
    low_ref[:, HD:] = total[:, HD:].astype(jnp.bfloat16)


def finish_group(sums, arrived, cosine, sine, index):
    rows = arrived[0].shape[0]
    tile = min(256, rows)
    skip = index * (rows // tile)
    wide = pl.BlockSpec((tile, 2 * HD), lambda g: (g, 0))
    half = pl.BlockSpec((tile, HD // 2), lambda g: (skip + g, 0))
    return pl.pallas_call(
        finish_group_kernel,
        out_shape=jax.ShapeDtypeStruct((rows, 2 * HD), jnp.bfloat16),
        grid=(rows // tile,),
        in_specs=[half, half, pl.BlockSpec((tile, 2 * HD), lambda g: (skip + g, 0))] + [wide] * len(arrived),
        out_specs=wide,
        cost_estimate=SMALL,
        name="finish_group",
    )(cosine, sine, sums, *arrived)


ROW = 64
TILE = 256
WIDE = 768
GATE_TILE = 384


def pick(middle, total_ref, outward_ref, rows):
    total = jnp.where(middle, total_ref[rows, :].astype(jnp.float32), outward_ref[rows, :].astype(jnp.float32))
    return total


def fold(values):
    return jnp.sum(values.reshape(-1, 8, values.shape[1]), axis=0)


def gate_kernel(number, chunk, middle_ref, *rest):
    came, rest = rest[: 2 * number], rest[2 * number :]
    hidden_ref, gains_ref, gate_weight_ref, up_weight_ref, *rest = rest
    attended_ref, between_ref, normed_ref, gate_ref, up_ref, mixed_ref = rest
    middle = middle_ref[0] == 1

    @pl.when(pl.program_id(0) == 0)
    def _():
        for i in range(number):

            def step(r, carry):
                rows = pl.ds(pl.multiple_of(r * ROW, ROW), ROW)
                place = pl.ds(pl.multiple_of(i * chunk + r * ROW, ROW), ROW)
                attended = pick(middle, came[2 * i], came[2 * i + 1], rows)
                between = hidden_ref[place, :].astype(jnp.float32) + scaled(attended)[1] * gains_ref[1:2, :]
                attended_ref[place, :] = attended.astype(jnp.bfloat16)
                between_ref[place, :] = between
                normed_ref[place, :] = (scaled(between)[1] * gains_ref[2:3, :]).astype(jnp.bfloat16)
                return carry

            lax.fori_loop(0, chunk // ROW, step, 0)

    gate = jnp.dot(normed_ref[...], gate_weight_ref[...], preferred_element_type=jnp.float32)
    up = jnp.dot(normed_ref[...], up_weight_ref[...], preferred_element_type=jnp.float32)
    gate_ref[...] = gate
    up_ref[...] = up
    mixed_ref[...] = (jax.nn.gelu(gate, approximate=True) * up).astype(jnp.bfloat16)


def full_block(rows, columns):
    return pl.BlockSpec((rows, columns), lambda n, m: (0, 0))


def gate_call(middle, came, hidden, gains, gate_weight, up_weight, pair):
    number = len(came) // 2
    chunk, features = came[0].shape
    rows = number * chunk
    units = gate_weight.shape[1]
    wide = pl.BlockSpec((features, GATE_TILE), lambda n, m: (0, n))
    tall = pl.BlockSpec((rows, GATE_TILE), lambda n, m: (0, n))
    return pl.pallas_call(
        functools.partial(gate_kernel, number, chunk),
        out_shape=(
            jax.ShapeDtypeStruct((rows, features), jnp.bfloat16),
            jax.ShapeDtypeStruct((rows, features), jnp.float32),
            jax.ShapeDtypeStruct((rows, features), jnp.bfloat16),
            jax.ShapeDtypeStruct((rows, units), jnp.float32),
            jax.ShapeDtypeStruct((rows, units), jnp.float32),
            jax.ShapeDtypeStruct((rows, units), jnp.bfloat16),
        ),
        grid_spec=pltpu.PrefetchScalarGridSpec(
            num_scalar_prefetch=1,
            grid=(units // GATE_TILE,),
            in_specs=[full_block(chunk, features)] * len(came)
            + [pl.BlockSpec((rows, features), lambda n, m: (pair, 0)), full_block(4, features), wide, wide],
            out_specs=[full_block(rows, features)] * 3 + [tall] * 3,
        ),
        compiler_params=pltpu.CompilerParams(vmem_limit_bytes=60 * 2**20),
        cost_estimate=SMALL,
        name="gate",
    )(middle, *came, hidden, gains, gate_weight, up_weight)


def back_out_kernel(number, chunk, *rest):
    terms, outs = rest[:-number], rest[-number:]
    total = 0.0
    for left, weight in zip(terms[::2], terms[1::2]):
        total = total + lax.dot_general(left[...], weight[...], NT, preferred_element_type=jnp.float32)
    total = total.astype(jnp.bfloat16)
    for i, out in enumerate(outs):
        out[...] = total[i * chunk : (i + 1) * chunk]


def back_out(terms, chunk):
    rows, units = terms[0][0].shape
    features = terms[0][1].shape[0]
    number = rows // chunk
    left = pl.BlockSpec((rows, units), lambda n: (0, 0))
    weight = pl.BlockSpec((WIDE, units), lambda n: (n, 0))
    return pl.pallas_call(
        functools.partial(back_out_kernel, number, chunk),
        out_shape=[jax.ShapeDtypeStruct((chunk, features), jnp.bfloat16)] * number,
        grid=(features // WIDE,),
        in_specs=[left, weight] * len(terms),
        out_specs=[pl.BlockSpec((chunk, WIDE), lambda n: (0, n))] * number,
        compiler_params=pltpu.CompilerParams(vmem_limit_bytes=48 * 2**20),
        cost_estimate=SMALL,
        name="back_out",
    )(*[array for term in terms for array in term])


def mixed_back_kernel(number, chunk, middle_ref, *rest):
    came, rest = rest[: 2 * number], rest[2 * number :]
    between_ref, upstream_ref, gains_ref, down_ref, gate_ref, up_ref, *rest = rest
    result_ref, fed_ref, gain_ref, gate_low_ref, up_low_ref = rest[-5:]
    middle = middle_ref[0] == 1

    @pl.when(pl.program_id(0) == 0)
    def _():
        gain_ref[...] = jnp.zeros_like(gain_ref)
        for i in range(number):

            def step(r, carry):
                rows = pl.ds(pl.multiple_of(r * ROW, ROW), ROW)
                place = pl.ds(pl.multiple_of(i * chunk + r * ROW, ROW), ROW)
                factor, normed = scaled(pick(middle, came[2 * i], came[2 * i + 1], rows))
                raised = normed * gains_ref[3:4, :]
                result_ref[place, :] = (between_ref[place, :] + raised).astype(jnp.bfloat16)
                given = upstream_ref[place, :].astype(jnp.float32)
                gain_ref[...] += fold(given * normed)
                inner = jnp.mean(given * raised, axis=-1, keepdims=True)
                fed_ref[place, :] = (factor * (given * gains_ref[3:4, :] - normed * inner)).astype(jnp.bfloat16)
                return carry

            lax.fori_loop(0, chunk // ROW, step, 0)

    mixed_grad = jnp.dot(fed_ref[...], down_ref[...], preferred_element_type=jnp.float32)
    gate = gate_ref[...]
    inside = GELU * (gate + 0.044715 * gate * gate * gate)
    bent = jnp.tanh(inside)
    half = 0.5 * (1.0 + bent)
    slope = half + 0.5 * gate * (1.0 - bent * bent) * (GELU * (1.0 + 3 * 0.044715 * gate * gate))
    gate_low_ref[...] = (mixed_grad * up_ref[...] * slope).astype(jnp.bfloat16)
    up_low_ref[...] = (mixed_grad * (gate * half)).astype(jnp.bfloat16)


def mixed_back(middle, came, between, upstream, gains, down_weight, gate, up, pair, before):
    number = len(came) // 2
    chunk, features = came[0].shape
    rows = number * chunk
    units = down_weight.shape[1]
    tall = pl.BlockSpec((rows, GATE_TILE), lambda n, m: (0, n))
    extra = [] if before is None else [before]
    return pl.pallas_call(
        functools.partial(mixed_back_kernel, number, chunk),
        out_shape=(
            jax.ShapeDtypeStruct(upstream.shape, jnp.bfloat16),
            jax.ShapeDtypeStruct((rows, features), jnp.bfloat16),
            jax.ShapeDtypeStruct((8, features), jnp.float32),
            jax.ShapeDtypeStruct((rows, units), jnp.bfloat16),
            jax.ShapeDtypeStruct((rows, units), jnp.bfloat16),
        ),
        grid_spec=pltpu.PrefetchScalarGridSpec(
            num_scalar_prefetch=1,
            grid=(units // GATE_TILE,),
            in_specs=[full_block(chunk, features)] * len(came)
            + [
                full_block(rows, features),
                pl.BlockSpec((rows, features), lambda n, m: (pair, 0)),
                full_block(4, features),
                pl.BlockSpec((features, GATE_TILE), lambda n, m: (0, n)),
                tall,
                tall,
            ]
            + [pl.BlockSpec(memory_space=pl.ANY)] * len(extra),
            out_specs=[pl.BlockSpec((rows, features), lambda n, m: (pair, 0)), full_block(rows, features)]
            + [full_block(8, features)]
            + [tall] * 2,
        ),
        input_output_aliases={} if before is None else {len(came) + 7: 0},
        compiler_params=pltpu.CompilerParams(vmem_limit_bytes=60 * 2**20),
        cost_estimate=SMALL,
        name="mixed_back",
    )(middle, *came, between, upstream, gains, down_weight, gate, up, *extra)


def attention_low_kernel(middle_ref, *rest):
    came, rest = rest[:4], rest[4:]
    (between_ref, attended_ref, upstream_ref, gains_ref, weight_ref,
     grad_ref, low_ref, gain_two_ref, gain_three_ref, heads_ref) = rest
    middle = middle_ref[0] == 1
    step = pl.program_id(0)
    early = step < pl.num_programs(0) // 2
    size = between_ref.shape[0]

    @pl.when(step == 0)
    def _():
        gain_two_ref[...] = jnp.zeros_like(gain_two_ref)
        gain_three_ref[...] = jnp.zeros_like(gain_three_ref)

    rows = pl.ds(0, size)
    total = jnp.where(early, pick(middle, came[0], came[1], rows), pick(middle, came[2], came[3], rows))
    factor, normed = scaled(between_ref[...])
    gain_three_ref[...] += fold(total * normed)
    raised = total * gains_ref[2:3, :]
    inner = jnp.mean(raised * normed, axis=-1, keepdims=True)
    grad = upstream_ref[...].astype(jnp.float32) + factor * (raised - normed * inner)
    grad_ref[...] = grad
    factor, normed = scaled(attended_ref[...].astype(jnp.float32))
    gain_two_ref[...] += fold(grad * normed)
    raised = grad * gains_ref[1:2, :]
    inner = jnp.mean(raised * normed, axis=-1, keepdims=True)
    low_ref[pl.ds(pl.multiple_of(step * size, size), size), :] = (factor * (raised - normed * inner)).astype(jnp.bfloat16)

    @pl.when(step == pl.num_programs(0) - 1)
    def _():
        heads = jnp.dot(low_ref[...], weight_ref[...], preferred_element_type=jnp.float32)
        heads_ref[...] = heads.astype(jnp.bfloat16)


def attention_low(middle, came, between, attended, upstream, gains, weight, index):
    chunk, features = between.shape
    width = weight.shape[1]
    size = ROW
    parts = chunk // size

    def some(offset):
        return pl.BlockSpec((size, features), lambda n, m: (offset * parts + n, 0))

    first = pl.BlockSpec((size, features), lambda n, m: (jnp.minimum(n, parts // 2 - 1), 0))
    second = pl.BlockSpec((size, features), lambda n, m: (jnp.maximum(n - parts // 2, 0), 0))
    return pl.pallas_call(
        attention_low_kernel,
        out_shape=(
            jax.ShapeDtypeStruct((chunk, features), jnp.float32),
            jax.ShapeDtypeStruct((chunk, features), jnp.bfloat16),
            jax.ShapeDtypeStruct((8, features), jnp.float32),
            jax.ShapeDtypeStruct((8, features), jnp.float32),
            jax.ShapeDtypeStruct((chunk, width), jnp.bfloat16),
        ),
        grid_spec=pltpu.PrefetchScalarGridSpec(
            num_scalar_prefetch=1,
            grid=(parts,),
            in_specs=[
                first, first, second, second, some(0), some(0), some(index), full_block(4, features),
                full_block(features, width),
            ],
            out_specs=[
                some(0), full_block(chunk, features), full_block(8, features), full_block(8, features),
                full_block(chunk, width),
            ],
        ),
        compiler_params=pltpu.CompilerParams(vmem_limit_bytes=48 * 2**20),
        cost_estimate=SMALL,
        name="attention_low",
    )(middle, *came, between, attended, upstream, gains, weight)


def share_kernel(number, *rest):
    lefts, rights, (out_ref, turned_ref, right_ref, sems) = rest[:number], rest[number : 2 * number], rest[2 * number :]
    rows = lefts[0].shape[0]

    @pl.when(pl.program_id(0) == 0)
    def _():
        load_pieces(rights, right_ref, sems)

    for i, left in enumerate(lefts):
        turned_ref[:, i * rows : (i + 1) * rows] = left[...].T
    out = jnp.dot(turned_ref[...], right_ref[...], preferred_element_type=jnp.float32)
    out_ref[...] = out.astype(jnp.bfloat16)


def share_call(lefts, rights):
    number = len(rights)
    rows, columns = rights[0].shape
    features = lefts[0].shape[1]
    cut = len(lefts) == 1 and number > 1
    lefts = lefts * number if cut else lefts
    return pl.pallas_call(
        functools.partial(share_kernel, number),
        out_shape=jax.ShapeDtypeStruct((features, columns), jnp.bfloat16),
        grid=(features // TILE,),
        in_specs=[pl.BlockSpec((rows, TILE), lambda n, i=i * cut: (i, n)) for i in range(number)]
        + [pl.BlockSpec(memory_space=pl.ANY)] * number,
        out_specs=pl.BlockSpec((TILE, columns), lambda n: (n, 0)),
        scratch_shapes=[
            pltpu.VMEM((TILE, number * rows), jnp.bfloat16),
            pltpu.VMEM((number * rows, columns), jnp.bfloat16),
            pltpu.SemaphoreType.DMA((number,)),
        ],
        compiler_params=pltpu.CompilerParams(vmem_limit_bytes=48 * 2**20),
        cost_estimate=SMALL,
        name="share",
    )(*lefts, *rights)


def pair_sums_kernel(*refs):
    number = len(refs) // 3
    for i in range(number):
        left, right, out = refs[2 * i], refs[2 * i + 1], refs[2 * number + i]
        out[...] = (left[...].astype(jnp.float32) + right[...].astype(jnp.float32)).astype(jnp.bfloat16)


def pair_sums(pairs):
    rows, columns = pairs[0][0].shape
    tile = min(rows, ROW)
    block = pl.BlockSpec((tile, columns), lambda g: (g, 0))
    return pl.pallas_call(
        pair_sums_kernel,
        out_shape=[jax.ShapeDtypeStruct((rows, columns), jnp.bfloat16)] * len(pairs),
        grid=(rows // tile,),
        in_specs=[block] * (2 * len(pairs)),
        out_specs=[block] * len(pairs),
        cost_estimate=SMALL,
        name="pair_sums",
    )(*[array for pair in pairs for array in pair])


def linear_back_kernel(query_grad_ref, group_ref, query_ref, weight_ref, hidden_ref, factor_ref, one_ref, two_ref, gain_ref):
    partial = lax.dot_general(query_grad_ref[...], query_ref[...], NT, preferred_element_type=jnp.float32)
    partial += lax.dot_general(group_ref[...], weight_ref[...], NT, preferred_element_type=jnp.float32)
    normed = hidden_ref[...].astype(jnp.float32) * factor_ref[:, :1]
    gain_ref[...] = fold(partial * normed)
    half = one_ref.shape[0]
    partial = partial.astype(jnp.bfloat16)
    one_ref[...] = partial[:half]
    two_ref[...] = partial[half:]


def linear_back(query_grad, query_block, group, group_block, query_weight, group_weight, hidden, factor, index, rows):
    features, width = query_weight.shape
    tile = WIDE
    row = pl.BlockSpec((rows, tile), lambda n: (index, n))
    weight = pl.BlockSpec((tile, width), lambda n: (n, 0))
    half = pl.BlockSpec((rows // 2, tile), lambda n: (0, n))
    return pl.pallas_call(
        linear_back_kernel,
        out_shape=(
            jax.ShapeDtypeStruct((rows // 2, features), jnp.bfloat16),
            jax.ShapeDtypeStruct((rows // 2, features), jnp.bfloat16),
            jax.ShapeDtypeStruct((8, features), jnp.float32),
        ),
        grid=(features // tile,),
        in_specs=[
            pl.BlockSpec((rows, width), lambda n: (query_block, 0)),
            pl.BlockSpec((rows, width), lambda n: (group_block, 0)),
            weight,
            weight,
            row,
            pl.BlockSpec((rows, 128), lambda n: (index, 0)),
        ],
        out_specs=[half, half, pl.BlockSpec((8, tile), lambda n: (0, n))],
        compiler_params=pltpu.CompilerParams(vmem_limit_bytes=32 * 2**20),
        cost_estimate=SMALL,
        name="linear_back",
    )(query_grad, group, query_weight, group_weight, hidden, factor)


def input_grad_kernel(middle_ref, *rest):
    came, (hidden_ref, upper_ref, gains_ref, *ignored, out_ref) = rest[:4], rest[4:]
    middle = middle_ref[0] == 1
    early = pl.program_id(0) < pl.num_programs(0) // 2
    rows = pl.ds(0, hidden_ref.shape[0])
    total = jnp.where(early, pick(middle, came[0], came[1], rows), pick(middle, came[2], came[3], rows))
    factor, normed = scaled(hidden_ref[...].astype(jnp.float32))
    raised = total * gains_ref[0:1, :]
    inner = jnp.mean(raised * normed, axis=-1, keepdims=True)
    out_ref[...] = upper_ref[...] + factor * (raised - normed * inner)


def input_grad(middle, came, hidden, upper, upper_block, gains, index, before):
    half, features = came[0].shape
    size = min(ROW, half)
    parts = 2 * half // size

    def some(block):
        return pl.BlockSpec((size, features), lambda n, m: (block * parts + n, 0))

    first = pl.BlockSpec((size, features), lambda n, m: (jnp.minimum(n, parts // 2 - 1), 0))
    second = pl.BlockSpec((size, features), lambda n, m: (jnp.maximum(n - parts // 2, 0), 0))
    extra = [] if before is None else [before]
    return pl.pallas_call(
        input_grad_kernel,
        out_shape=jax.ShapeDtypeStruct(hidden.shape, jnp.float32),
        grid_spec=pltpu.PrefetchScalarGridSpec(
            num_scalar_prefetch=1,
            grid=(parts,),
            in_specs=[first, first, second, second, some(index), some(upper_block), full_block(4, features)]
            + [pl.BlockSpec(memory_space=pl.ANY)] * len(extra),
            out_specs=some(index),
        ),
        input_output_aliases={8: 0} if extra else {},
        compiler_params=pltpu.CompilerParams(vmem_limit_bytes=32 * 2**20),
        cost_estimate=SMALL,
        name="input_grad",
    )(middle, *came, hidden, upper, gains, *extra)


THETA = 10000.0
ROWS = ("dp", "seq")
LINE = "tensor"
LOW = jnp.bfloat16
FULL = jnp.float32
CHUNK = 512
FINE = 256
BUDGET = 48.0
FINE_BUDGET = 30.0
(HEADS, STAT, ATTENDED, BETWEEN, NORMED, GATE, UP, MIXED, FED, RESULT, FED_LOW, GAIN_ONE, GAIN_TWO, GAIN_THREE,
 GAIN_FOUR, GATE_LOW, UP_LOW, NORMED_GRAD, MIDDLE_GRAD, ATTENTION_LOW, QUERY_GRAD, SUMS, SPREAD, GROUP,
 LINEAR, INPUT_GRAD, SHARE, BESIDE, PASSED, BELOW, TOTAL) = range(31)
DOWN_SHARE, GATE_SHARE, UP_SHARE, LINEAR_SHARE = range(4)


def dot(a, b, dims=(((1,), (0,)), ((), ()))):
    return lax.dot_general(a, b, dims, preferred_element_type=FULL)


def angles(places, width):
    half = width // 2
    frequency = jnp.power(THETA, -2.0 * jnp.arange(half, dtype=FULL) / width)
    turned = places.astype(FULL)[:, None] * frequency[None, :]
    return (jnp.cos(turned), jnp.sin(turned))


def gather(weight):
    return lax.all_gather(weight, ROWS, axis=0, tiled=True)


def scatter(grad):
    return lax.psum_scatter(grad, ROWS, scatter_dimension=0, tiled=True)


def hop_by(array, hop, seqs):
    return lax.ppermute(array, "seq", [(i, i + hop) for i in range(seqs - hop)])


def hop_back(array, hop, seqs):
    return lax.ppermute(array, "seq", [(i + hop, i) for i in range(seqs - hop)])


def cut(array, pieces):
    size = array.shape[0] // pieces
    return [array[i * size : (i + 1) * size] for i in range(pieces)]


def fetch_window(own, reach, seqs, later):
    if seqs != 4 or reach != 2:
        return [hop_by(own, hop, seqs) for hop in range(reach, 0, -1)]
    near, far = [], []
    last = lax.axis_index("seq") == 2
    pieces = cut(own, 4)
    pieces[3] = lax.optimization_barrier((pieces[3], later()))[0]
    for piece in pieces:
        beside = lax.ppermute(piece, "seq", [(0, 1), (2, 3)])
        below = lax.ppermute(piece, "seq", [(0, 2), (1, 3)])
        passed = lax.ppermute(below, "seq", [(3, 2)])
        near.append((beside, passed))
        far.append(below)
    return [far, [jnp.where(last, passed, beside) for beside, passed in near]]


class Schedule:
    def __init__(self, token, count):
        self.count = count
        self.token = token
        self.values = {}
        self.ready = {}
        self.jobs = []
        self.lines = [[], []]
        self.entered = []
        self.stages = [[None, None, None], [None, None, None]]
        self.now = 0
        self.late = []

    def job(self, cost, needs, work):
        self.jobs.append((cost, needs, work))

    def enter(self, name, halves):
        self.entered.append((name, halves))

    def after(self, *arrays):
        return lax.optimization_barrier((arrays, self.token))[0]

    def barrier(self, *arrays):
        self.token, arrays = lax.optimization_barrier((self.token, arrays))
        return arrays

    def move(self, half, arrived):
        inward, across, outward = (
            None if item is None else (item[0],) + tuple(two) for item, two in zip(self.stages[half], arrived)
        )
        moved = [None, None, None]
        if self.lines[half]:
            name, part = self.lines[half].pop(0)
            moved[0] = (name, part, lax.ppermute(part, LINE, [(0, 1), (3, 2)]))
        pairs = [item[1:] for item in (inward, across) if item is not None]
        sums = list(pair_sums(pairs)) if pairs and pairs[0][0].shape == pairs[-1][0].shape else [
            pair_sums([pair])[0] for pair in pairs]
        if inward is not None:
            pair = sums.pop(0)
            moved[1] = (inward[0], pair, lax.ppermute(pair, LINE, [(1, 2), (2, 1)]))
        if across is not None:
            total = sums.pop(0)
            moved[2] = (across[0], total, lax.ppermute(total, LINE, [(1, 0), (2, 3)]))
        self.stages[half] = moved
        return outward

    def tick(self, budget):
        made, spent, left = {}, 0.0, []
        for cost, needs, work in self.jobs:
            fits = spent == 0.0 or spent + cost <= budget
            if fits and all(self.ready.get(need, self.now + 1) <= self.now for need in needs):
                made.update(work())
                spent += cost
            else:
                left.append((cost, needs, work))
        self.jobs = left
        late = [item for item in self.late if item[1] <= self.now]
        self.late = [item for item in self.late if item[1] > self.now]
        entered, self.entered = self.entered, []
        waiting = [[None if item is None else item[1:] for item in stages] for stages in self.stages]
        made, halves, brought, first = self.barrier(
            made, [item[1] for item in entered], [item[2] for item in late], waiting[0]
        )
        for (name, ignored), (one, two) in zip(entered, halves):
            self.lines[0].append((name, one))
            self.lines[1].append((name, two))
        one = self.move(0, first)
        (second,) = self.barrier(waiting[1])
        two = self.move(1, second)
        if one is not None:
            made[one[0]] = one[1:] + two[1:]
        for item, value in zip(late, brought):
            made[item[0]] = value
        self.now += 1
        for name, value in made.items():
            self.values[name] = value
            self.ready[name] = self.now

    def run(self):
        while self.jobs or self.late or any(self.lines) or any(any(stages) for stages in self.stages):
            self.tick(FINE_BUDGET if self.ready.get((SUMS, self.count), self.now + 1) <= self.now else BUDGET)


def per_device(
    inputs,
    positions,
    query_weight,
    key_weight,
    value_weight,
    output_weight,
    gate_weight,
    up_weight,
    down_weight,
    pre_attention,
    post_attention,
    pre_feedforward,
    post_feedforward,
    cotangent,
):
    hidden = inputs[0]
    upstream = cotangent[0]
    places = positions[0]
    rows, features = hidden.shape
    chunk = min(CHUNK, rows)
    count = rows // chunk
    fine = min(FINE, chunk)
    fines = rows // fine
    split = chunk // fine
    seqs = lax.axis_size("seq")
    reach = min((WINDOW + rows - 2) // rows, seqs - 1)
    heads_width = query_weight.shape[1]
    group_width = key_weight.shape[1]

    gains = jnp.stack([pre_attention, post_attention, pre_feedforward, post_feedforward], axis=1)
    gains = jnp.pad(gains, ((0, 0), (0, 124)))
    packed = gather(jnp.concatenate([key_weight, value_weight, gains], axis=1))
    group_full = packed[:, : 2 * group_width]
    gains = 1.0 + packed[:, 2 * group_width : 2 * group_width + 4].astype(FULL).T
    query_weight, output_weight, packed = lax.optimization_barrier((query_weight, output_weight, packed))
    query_full = gather(query_weight)
    output_full = gather(output_weight)

    cosine, sine = angles(places, HD)
    normed_one, own, factor = project_group(hidden, gains[:1], group_full, cosine, sine)
    query_low = project_heads(normed_one, query_full, cosine, sine)
    fetched = fetch_window(own, reach, seqs, lambda: query_low)
    low, bounds = limits(places, chunk)
    low_wide = jnp.broadcast_to(low[:, None], (rows, 128))
    low_row = low[None, :]
    fetched, query_low, low_wide, low_row, bounds, gate_weight, up_weight, down_weight = lax.optimization_barrier(
        (fetched, query_low, low_wide, low_row, bounds, gate_weight, up_weight, down_weight)
    )
    blocks = []
    for block in fetched:
        blocks += block if isinstance(block, list) else [block]
    blocks += cut(own, rows // blocks[0].shape[0])
    gate_full = gather(gate_weight)
    up_full = gather(up_weight)
    down_full = gather(down_weight)

    place = lax.axis_index(LINE)
    middle = ((place == 1) | (place == 2)).astype(jnp.int32)[None]
    plan = Schedule(bounds[0, 0], count)
    values = plan.values

    def part(array, index, size=chunk):
        return array[index * size : (index + 1) * size]

    def every(kind, number):
        return [values[kind, i] for i in range(number)]

    def attend_job(i):
        def work():
            (query,) = plan.after(query_low)
            head, stat = attend(query, blocks, low_wide, bounds, i, 1, chunk)
            plan.enter((ATTENDED, i), back_out([(head, output_full)], chunk // 2))
            return {(HEADS, i): head, (STAT, i): stat}

        plan.job(12.0 if i else 40.0, [], work)

    def forward_job(i):
        def work():
            kinds = (ATTENDED, BETWEEN, NORMED, GATE, UP, MIXED)
            made = gate_call(middle, values[ATTENDED, i], hidden, gains, gate_full, up_full, i)
            plan.enter((FED, i), back_out([(made[5], down_full)], chunk // 2))
            return {(kind, i): array for kind, array in zip(kinds, made)}

        plan.job(36.0, [(ATTENDED, i)], work)

    def backward_job(i):
        def work():
            kinds = (RESULT, FED_LOW, GAIN_FOUR, GATE_LOW, UP_LOW)
            made = mixed_back(
                middle, values[FED, i], values[BETWEEN, i], upstream, gains, down_full,
                values[GATE, i], values[UP, i], i, values.get((RESULT, 0)),
            )
            values[RESULT, 0] = made[0]
            plan.enter((NORMED_GRAD, i), back_out([(made[3], gate_full), (made[4], up_full)], chunk // 2))
            return {(kind, i): array for kind, array in zip(kinds[1:], made[1:])}

        plan.job(40.0, [(FED, i)], work)

    def attention_job(i):
        def work():
            kinds = (MIDDLE_GRAD, ATTENTION_LOW, GAIN_TWO, GAIN_THREE)
            *made, heads_grad = attention_low(
                middle, values[NORMED_GRAD, i], values[BETWEEN, i], values[ATTENDED, i], upstream, gains, output_full, i
            )
            query_grad, *sums = attend_back(
                query_low, heads_grad, values[HEADS, i], values[STAT, i], blocks, low_row,
                cosine, sine, bounds, values.get((SUMS, i)), i, 1, chunk, sent if i == count - 1 else (),
            )
            made = {(kind, i): array for kind, array in zip(kinds, made)}
            made.update({(QUERY_GRAD, i): query_grad, (SUMS, i + 1): sums[-1]})
            made.update({(SPREAD, k): array for k, array in enumerate(sums[:-1])})
            return made

        plan.job(44.0, [(NORMED_GRAD, i)] + ([(SUMS, i)] if i else []), work)

    def first_spread_job():
        def work():
            for k in range(4):
                near = values[SPREAD, 4 + k]
                beside = lax.ppermute(near, "seq", [(1, 0), (3, 2)])
                passed = lax.ppermute(near, "seq", [(2, 3)])
                plan.late.append(((BESIDE, k), plan.now + k // 2 + 1, beside))
                plan.late.append(((PASSED, k), plan.now + k // 2, passed))
            return {}

        plan.job(1.0, [(SUMS, count)], work)

    def second_spread_job(k):
        def work():
            (below,) = pair_sums([(values[SPREAD, k], values[PASSED, k])])
            plan.late.append(((BELOW, k), plan.now, lax.ppermute(below, "seq", [(2, 0), (3, 1)])))
            return {}

        plan.job(1.0, [(PASSED, k)], work)

    def hops_job():
        def work():
            for hop in range(1, reach + 1):
                plan.late.append(((BESIDE, hop), plan.now + 1, hop_back(values[SPREAD, reach - hop], hop, seqs)))
            return {}

        plan.job(1.0, [(SUMS, count)], work)

    def group_job(k, needs):
        def work():
            arrived = [values[need] for need in needs]
            group = finish_group(values[SUMS, count], arrived, cosine, sine, k)
            made = {(GROUP, k): group}
            each = fines // groups
            for i in range(k * each, (k + 1) * each):
                *halves, made[GAIN_ONE, i] = linear_back(
                    values[QUERY_GRAD, i // split], i % split, group, i - k * each, query_full, group_full,
                    hidden, factor, i, fine,
                )
                plan.enter((LINEAR, i), halves)
            return made

        plan.job(3.0 + 5.0 * fines // groups, needs, work)

    def input_job(i):
        def work():
            values[INPUT_GRAD, 0] = input_grad(
                middle, values[LINEAR, i], hidden, values[MIDDLE_GRAD, i // split], i % split, gains, i,
                values.get((INPUT_GRAD, 0)),
            )
            return {}

        plan.job(4.0, [(LINEAR, i)], work)

    def share_job(index, cost, needs, left, right):
        def work():
            lefts = left()
            lefts[0], = plan.after(lefts[0])
            return {(SHARE, index): share_call(lefts, right())}

        plan.job(cost, needs, work)

    def scatter_job(index, ticks, needs):
        def work():
            (share,) = plan.after(values[SHARE, index])
            plan.late.append(((TOTAL, index), plan.now + ticks - 1, scatter(share)))
            return {}

        plan.job(0.0, [(SHARE, index)] + needs, work)

    def linear_share_job():
        def work():
            kinds = ((GAIN_ONE, fines), (GAIN_TWO, count), (GAIN_THREE, count), (GAIN_FOUR, count))
            columns = jnp.stack([jnp.sum(sum(every(*kind)), axis=0) for kind in kinds], axis=1)
            columns = jnp.pad(columns.astype(LOW), ((0, 0), (0, 124)))
            (left,) = plan.after(normed_one)
            grads = [share_call([left], every(QUERY_GRAD, count)), share_call([left], every(GROUP, groups))]
            grads.append(share_call(every(ATTENTION_LOW, count), every(HEADS, count)))
            return {(SHARE, LINEAR_SHARE): jnp.concatenate(grads + [columns], axis=1)}

        plan.job(30.0, [(GAIN_ONE, i) for i in range(fines)], work)

    square = seqs == 4 and reach == 2
    groups = 4 if square else 1
    sent = (rows // 4,) * 8 if square else (rows,) * reach
    for i in range(count):
        attend_job(i)
    for i in range(count):
        forward_job(i)
    for i in range(count):
        backward_job(i)
    for i in range(count):
        attention_job(i)
    if square:
        first_spread_job()
        for k in range(4):
            second_spread_job(k)
        for k in range(4):
            group_job(k, [(BESIDE, k), (BELOW, k)])
    else:
        hops_job()
        group_job(0, [(BESIDE, hop) for hop in range(1, reach + 1)])
    backs = [(GATE_LOW, i) for i in range(count)] + [(SUMS, count)]
    share_job(DOWN_SHARE, 26.0, backs, lambda: every(FED_LOW, count), lambda: every(MIXED, count))
    share_job(GATE_SHARE, 26.0, backs, lambda: every(NORMED, count), lambda: every(GATE_LOW, count))
    share_job(UP_SHARE, 26.0, backs, lambda: every(NORMED, count), lambda: every(UP_LOW, count))
    linear_share_job()
    scatter_job(DOWN_SHARE, 3, [(GROUP, 0)] if groups == 1 else [(BELOW, 1)])
    scatter_job(GATE_SHARE, 3, [(TOTAL, DOWN_SHARE)])
    scatter_job(UP_SHARE, 3, [(TOTAL, GATE_SHARE)])
    scatter_job(LINEAR_SHARE, 2, [(TOTAL, UP_SHARE)])
    for i in range(fines):
        input_job(i)
    plan.run()

    shares = [array.astype(FULL) for array in every(TOTAL, 4)]
    linear_share = shares[LINEAR_SHARE]
    width = heads_width + 2 * group_width
    gain_grads = linear_share[:, width + heads_width :][:, :4].T
    gain_one = gain_grads[0]
    for turn in (1, 2):
        gain_one = gain_one + lax.ppermute(gain_one, LINE, [(i, i ^ turn) for i in range(4)])
    return (
        values[RESULT, 0][None],
        values[INPUT_GRAD, 0][None],
        linear_share[:, :heads_width],
        linear_share[:, heads_width : heads_width + group_width],
        linear_share[:, heads_width + group_width : width],
        linear_share[:, width : width + heads_width],
        shares[GATE_SHARE],
        shares[UP_SHARE],
        shares[DOWN_SHARE],
        gain_one,
        gain_grads[1],
        gain_grads[2],
        gain_grads[3],
    )


def solution(mesh):
    tokens = P("dp", "seq", None)
    weight = P(ROWS, LINE)
    gain = P(ROWS)
    return jax.shard_map(
        per_device,
        mesh=mesh,
        in_specs=(tokens, P("dp", "seq")) + (weight,) * 7 + (gain,) * 4 + (tokens,),
        out_specs=(tokens, tokens) + (weight,) * 7 + (gain,) * 4,
        check_vma=False,
    )
```

time: 4640 us -> 1710 us (0.37)
  waiting for transfers between devices: 3280 us -> 322 us
  Pallas kernels: 0 us -> 835 us
  matrix products: 803 us -> 0 us
  starting transfers between devices: 1.28 us -> 382 us
  other arithmetic: 381 us -> 23.4 us
  blocking collectives: 57.9 us -> 0 us
    psum x4 -> x0, waiting for transfers between devices: 2380 us -> none  [the longest x1 629 us: per_device(): feedforward_out = lax.psum(feedforward_part, 'tensor')]
    pallas_call x0 -> x108, Pallas kernels: none -> 835 us  [the longest x48 175 us: pair_sums(): pl.pallas_call(pair_sums_kernel, out_shape=[jax.ShapeDtypeStruct((rows, c...]
    dot_general x49 -> x0, matrix products: 803 us -> none  [the longest x8 106 us: block_scores(): jnp.einsum('qgrd,tgd->grqt', query_block, window_keys, preferred_element_...]
    reduce_scatter x9 -> x4, waiting for transfers between devices: 701 us -> 35 us  [scatter(): return lax.psum_scatter(grad, ROWS, scatter_dimension=0, tiled=True)]
    ppermute x0 -> x146, starting transfers between devices: none -> 381 us  [the longest x40 213 us: move(): moved[0] = (name, part, lax.ppermute(part, LINE, [(0, 1), (3, 2)]))]
    ppermute x0 -> x146, waiting for transfers between devices: none -> 251 us  [the longest x40 91.2 us: move(): moved[2] = (across[0], total, lax.ppermute(total, LINE, [(1, 0), (2, 3)]))]
    all_gather x9 -> x6, waiting for transfers between devices: 194 us -> 34.3 us  [gather(): return lax.all_gather(weight, ROWS, axis=0, tiled=True)]
    reduce_sum x12 -> x4, other arithmetic: 155 us -> 0.23 us  [work(): jnp.sum(sum(every(*kind)), axis=0)]
  transfers between devices with their start and end apart: 22 -> 156, of which waited for: 18 -> 29; matrix products, arithmetic and copies ran while one was open for 12% -> 2% of each run, Pallas kernels for 0% -> 47%
where the time goes in v1:
time: 1710 us; the launch traced here: 1690 us
  Pallas kernels  835 us (49%)
  starting transfers between devices  382 us (22%)
  waiting for transfers between devices  322 us (19%)
  local copies, waits for them, and re-layouts  114 us (7%)
  other arithmetic  23.4 us (1%)
  between operations  17.3 us (1%)
    ppermute x40, starting transfers between devices, move(): moved[0] = (name, part, lax.ppermute(part, LINE, [(0, 1), (3, 2)]))  213 us
    pallas_call x48, Pallas kernels, pair_sums(): pl.pallas_call(pair_sums_kernel, out_shape=[jax.ShapeDtypeStruct((rows, c...  175 us
    pallas_call x6, Pallas kernels, share_call(): pl.pallas_call(functools.partial(share_kernel, number), out_shape=jax.Sha...  123 us
    pallas_call x12, Pallas kernels, back_out(): pl.pallas_call(functools.partial(back_out_kernel, number, chunk), out_sha...  108 us
    pallas_call x4, Pallas kernels, gate_call(): pl.pallas_call(functools.partial(gate_kernel, number, chunk), out_shape=(...  105 us
    unnamed x411, local copies, waits for them, and re-layouts  102 us
    pallas_call x4, Pallas kernels, mixed_back(): pl.pallas_call(functools.partial(mixed_back_kernel, number, chunk), out_s...  91.4 us
    ppermute x40, waiting for transfers between devices, move(): moved[2] = (across[0], total, lax.ppermute(total, LINE, [(1, 0), (2, 3)]))  91.2 us
  transfers between devices with their start and end apart: 156, of which 29 were waited for; matrix products, arithmetic and copies ran while one was open for 2% of the time, Pallas kernels for 47%

profile of v1, /device:TPU:0, one launch (start us, length us, event | category | flops | bytes accessed | tf_op | source)
XLA Modules:
  0.0 1693.8 jit_solution(11242269912396478006)
XLA Ops:
  12.0 34.3 %all-gather.7.cloned.1.call-done = bf16[2304,640]{1,0:T(8,128)(2,1)} async-done(((bf16[288,640]{1,0:T(8,128)(2,1)}), bf16[2304,640]{1,0:T(8,128)(2,1)}) %all-gather.7.cloned.1.call-update) | async-done | bytes 2949136 | tf_op jit(solution)/shard_map/all_gather | solution.py:783
  57.7 11.5 project_group.1
  97.0 11.0 collective-permute-done.1.rest_1_
  237.1 10.5 collective-permute-done.14.refs_1_
  254.8 9.7 collective-permute-start.21
  279.0 19.1 %collective-permute-done.18.refs_1_ = bf16[256,2304]{1,0:T(8,128)(2,1)} collective-permute-done((bf16[256,2304]{1,0:T(8,128)(2,1)}, bf16[256,2304]{1,0:T(8,128)(2,1)}, u32[]{:S(2)}, u32[]{:S(2)}) %collective-permute-start.18) | collective-permute-done | bytes 1179680 | tf_op jit(solution)/shard_map/ppermute | solution.py:852
  312.0 11.4 collective-permute-done.21.refs_1_
  337.7 10.8 collective-permute-done.24.refs_1_
  349.9 26.1 %gate.4 = (bf16[512,2304]{1,0:T(8,128)(2,1)}, f32[512,2304]{1,0:T(8,128)}, bf16[512,2304]{1,0:T(8,128)(2,1)}, f32[512,2304]{1,0:T(8,128)}, f32[512,2304]{1,0:T(8,128)}, /*index=5*/bf16[512,2304]{1,0:T(8,128)(2,1)}) custom-call(s32[1]{0:T(128)} %bitcast.middle_ref, bf16[256,2304]{1,0:T(8,128)(2,1)} %get-tuple-element.756.rest_0_, ...), custom_call_target="tpu_custom_call" | custom-call | flops 1 | bytes 1 | tf_op jit(solution)/shard_map/gate/pallas_call | solution.py:418
  377.7 8.9 back_out.16
  413.0 26.1 %gate.5 = (bf16[512,2304]{1,0:T(8,128)(2,1)}, f32[512,2304]{1,0:T(8,128)}, bf16[512,2304]{1,0:T(8,128)(2,1)}, f32[512,2304]{1,0:T(8,128)}, f32[512,2304]{1,0:T(8,128)}, /*index=5*/bf16[512,2304]{1,0:T(8,128)(2,1)}) custom-call(s32[1]{0:T(128)} %bitcast.middle_ref, bf16[256,2304]{1,0:T(8,128)(2,1)} %get-tuple-element.787.rest_0_, ...), custom_call_target="tpu_custom_call" | custom-call | flops 1 | bytes 1 | tf_op jit(solution)/shard_map/gate/pallas_call | solution.py:418
  484.3 26.2 %gate.6 = (bf16[512,2304]{1,0:T(8,128)(2,1)}, f32[512,2304]{1,0:T(8,128)}, bf16[512,2304]{1,0:T(8,128)(2,1)}, f32[512,2304]{1,0:T(8,128)}, f32[512,2304]{1,0:T(8,128)}, /*index=5*/bf16[512,2304]{1,0:T(8,128)(2,1)}) custom-call(s32[1]{0:T(128)} %bitcast.middle_ref, bf16[256,2304]{1,0:T(8,128)(2,1)} %get-tuple-element.815.rest_0_, ...), custom_call_target="tpu_custom_call" | custom-call | flops 1 | bytes 1 | tf_op jit(solution)/shard_map/gate/pallas_call | solution.py:418
  512.1 8.9 back_out.18
  549.0 26.2 %gate.7 = (bf16[512,2304]{1,0:T(8,128)(2,1)}, f32[512,2304]{1,0:T(8,128)}, bf16[512,2304]{1,0:T(8,128)(2,1)}, f32[512,2304]{1,0:T(8,128)}, f32[512,2304]{1,0:T(8,128)}, /*index=5*/bf16[512,2304]{1,0:T(8,128)(2,1)}) custom-call(s32[1]{0:T(128)} %bitcast.middle_ref, bf16[256,2304]{1,0:T(8,128)(2,1)} %get-tuple-element.843.rest_0_, ...), custom_call_target="tpu_custom_call" | custom-call | flops 1 | bytes 1 | tf_op jit(solution)/shard_map/gate/pallas_call | solution.py:418
  576.8 8.8 back_out.19
  613.8 22.8 %mixed_back.4 = (bf16[2048,2304]{1,0:T(8,128)(2,1)}, bf16[512,2304]{1,0:T(8,128)(2,1)}, f32[8,2304]{1,0:T(8,128)}, bf16[512,2304]{1,0:T(8,128)(2,1)}, bf16[512,2304]{1,0:T(8,128)(2,1)}) custom-call(s32[1]{0:T(128)} %bitcast.middle_ref, bf16[256,2304]{1,0:T(8,128)(2,1)} %get-tuple-element.871.rest_0_, bf16[256,2304]{1,0:T(8,128)(2,1)} %collective-permute-done.44.rest_1_, ...), custom_call_target="tpu_custom_call" | custom-call | flops 1 | bytes 1 | tf_op jit(solution)/shard_map/mixed_back/pallas_call | solution.py:511
  638.2 16.1 back_out.20
  681.1 22.9 %mixed_back.5 = (bf16[2048,2304]{1,0:T(8,128)(2,1)}, bf16[512,2304]{1,0:T(8,128)(2,1)}, f32[8,2304]{1,0:T(8,128)}, bf16[512,2304]{1,0:T(8,128)(2,1)}, bf16[512,2304]{1,0:T(8,128)(2,1)}) custom-call(s32[1]{0:T(128)} %bitcast.middle_ref, bf16[256,2304]{1,0:T(8,128)(2,1)} %get-tuple-element.900.rest_0_, ...), custom_call_target="tpu_custom_call", output_to_operand_aliasing={{0}: (11, {})} | custom-call | flops 1 | bytes 1 | tf_op jit(solution)/shard_map/mixed_back/pallas_call | solution.py:511
  705.7 16.1 back_out.21
  742.6 10.2 collective-permute-done.59.rest_3_
  760.6 22.9 %mixed_back.6 = (bf16[2048,2304]{1,0:T(8,128)(2,1)}, bf16[512,2304]{1,0:T(8,128)(2,1)}, f32[8,2304]{1,0:T(8,128)}, bf16[512,2304]{1,0:T(8,128)(2,1)}, bf16[512,2304]{1,0:T(8,128)(2,1)}) custom-call(s32[1]{0:T(128)} %bitcast.middle_ref, bf16[256,2304]{1,0:T(8,128)(2,1)} %get-tuple-element.930.rest_0_, ...), custom_call_target="tpu_custom_call", output_to_operand_aliasing={{0}: (11, {})} | custom-call | flops 1 | bytes 1 | tf_op jit(solution)/shard_map/mixed_back/pallas_call | solution.py:511
  785.1 16.1 back_out.22
  827.0 22.9 %mixed_back.7 = (bf16[2048,2304]{1,0:T(8,128)(2,1)}, bf16[512,2304]{1,0:T(8,128)(2,1)}, f32[8,2304]{1,0:T(8,128)}, bf16[512,2304]{1,0:T(8,128)(2,1)}, bf16[512,2304]{1,0:T(8,128)(2,1)}) custom-call(s32[1]{0:T(128)} %bitcast.middle_ref, bf16[256,2304]{1,0:T(8,128)(2,1)} %get-tuple-element.951.rest_0_, ...), custom_call_target="tpu_custom_call", output_to_operand_aliasing={{0}: (11, {})} | custom-call | flops 1 | bytes 1 | tf_op jit(solution)/shard_map/mixed_back/pallas_call | solution.py:511
  852.9 16.1 back_out.23
  899.2 14.8 attention_low.4
  916.2 12.9 attend_back.4
  944.0 14.5 attention_low.5
  960.6 18.3 %attend_back.5 = (bf16[512,512]{1,0:T(8,128)(2,1)}, f32[6144,512]{1,0:T(8,128)}) custom-call(s32[4,2]{1,0:T(4,128)} %copy-done.151, bf16[2048,512]{1,0:T(8,128)(2,1)} %copy-done.11, bf16[512,512]{1,0:T(8,128)(2,1)} %copy-done.148, bf16[512,512]{1,0:T(8,128)(2,1)} %copy-done.69, f32[1024,128]{1,0:T(8,128)} %copy-done.145, ...), custom_call_target="tpu_custom_call" | custom-call | flops 1 | bytes 1 | tf_op jit(solution)/shard_map/attend_back/pallas_call | solution.py:217
  989.1 14.7 attention_low.6
  1005.9 20.8 %attend_back.6 = (bf16[512,512]{1,0:T(8,128)(2,1)}, f32[6144,512]{1,0:T(8,128)}) custom-call(s32[4,2]{1,0:T(4,128)} %copy-done.151, bf16[2048,512]{1,0:T(8,128)(2,1)} %copy-done.11, bf16[512,512]{1,0:T(8,128)(2,1)} %copy-done.149, bf16[512,512]{1,0:T(8,128)(2,1)} %copy-done.67, f32[1024,128]{1,0:T(8,128)} %copy-done.144, ...), custom_call_target="tpu_custom_call" | custom-call | flops 1 | bytes 1 | tf_op jit(solution)/shard_map/attend_back/pallas_call | solution.py:217
  1026.8 14.5 attention_low.7
  1043.4 21.0 %attend_back.7 = (bf16[512,512]{1,0:T(8,128)(2,1)}, bf16[512,512]{1,0:T(8,128)(2,1)}, bf16[512,512]{1,0:T(8,128)(2,1)}, bf16[512,512]{1,0:T(8,128)(2,1)}, bf16[5...) custom-call(s32[4,2]{1,0:T(4,128)} %copy-done.151, ...), custom_call_target="tpu_custom_call" | custom-call | flops 1 | bytes 1 | tf_op jit(solution)/shard_map/attend_back/pallas_call | solution.py:217
  1073.2 30.3 %share.6 = bf16[2304,2304]{1,0:T(8,128)(2,1)} custom-call(bf16[512,2304]{1,0:T(8,128)(2,1)S(1)} %copy-done.71, bf16[512,2304]{1,0:T(8,128)(2,1)S(1)} %copy-done.72, bf16[512,2304]{1,0:T(8,128)(2,1)} %get-tuple-element.1099.rest_2_, bf16[512,2304]{1,0:T(8,128)(2,1)} %get-tuple-element.1100.rest_3_, bf16[512,2304]{1,0:T(8,128)(2,1)} %get-tuple-element.1101.rest_0_.rest_4_, ...), custom_call_target="tpu_custom_call" | custom-call | flops 1 | bytes 1 | tf_op jit(solution)/shard_map/share/pallas_call | solution.py:636
  1119.3 30.3 %share.7 = bf16[2304,2304]{1,0:T(8,128)(2,1)} custom-call(bf16[512,2304]{1,0:T(8,128)(2,1)S(1)} %copy-done.30, bf16[512,2304]{1,0:T(8,128)(2,1)S(1)} %copy-done.32, bf16[512,2304]{1,0:T(8,128)(2,1)} %get-tuple-element.1111.rest_2_, bf16[512,2304]{1,0:T(8,128)(2,1)} %get-tuple-element.1112.rest_3_, bf16[512,2304]{1,0:T(8,128)(2,1)} %get-tuple-element.1113.rest_0_.rest_4_, ...), custom_call_target="tpu_custom_call" | custom-call | flops 1 | bytes 1 | tf_op jit(solution)/shard_map/share/pallas_call | solution.py:636
  1149.7 38.2 %collective-permute-done.91.rest_1_ = bf16[512,512]{1,0:T(8,128)(2,1)} collective-permute-done((bf16[512,512]{1,0:T(8,128)(2,1)}, bf16[512,512]{1,0:T(8,128)(2,1)}, u32[]{:S(2)}, u32[]{:S(2)}) %collective-permute-start.91) | collective-permute-done | bytes 524320 | tf_op jit(solution)/shard_map/ppermute | solution.py:1033
  1187.9 12.6 collective-permute-done.90.rest_1_
  1243.8 13.1 collective-permute-start.96
  1301.6 30.4 %share.8 = bf16[2304,2304]{1,0:T(8,128)(2,1)} custom-call(bf16[512,2304]{1,0:T(8,128)(2,1)S(1)} %copy-done.31, bf16[512,2304]{1,0:T(8,128)(2,1)S(1)} %copy-done.33, bf16[512,2304]{1,0:T(8,128)(2,1)} %get-tuple-element.1111.rest_2_, bf16[512,2304]{1,0:T(8,128)(2,1)} %get-tuple-element.1112.rest_3_, bf16[512,2304]{1,0:T(8,128)(2,1)} %get-tuple-element.1172.rest_2_.rest_4_, ...), custom_call_target="tpu_custom_call" | custom-call | flops 1 | bytes 1 | tf_op jit(solution)/shard_map/share/pallas_call | solution.py:636
  1333.7 10.1 share.11
  1359.7 11.1 share.9
  1377.1 10.5 share.10
  1393.7 24.6 %collective-permute-done.104.rest_1_ = bf16[128,2304]{1,0:T(8,128)(2,1)} collective-permute-done((bf16[128,2304]{1,0:T(8,128)(2,1)}, bf16[128,2304]{1,0:T(8,128)(2,1)}, u32[]{:S(2)}, u32[]{:S(2)}) %collective-permute-start.104) | collective-permute-done | bytes 589856 | tf_op jit(solution)/shard_map/ppermute | solution.py:861
  1432.9 9.2 collective-permute-start.114
  1457.7 11.8 collective-permute-done.116.rest_1_
  1469.5 11.1 collective-permute-done.119.rest_3_
  1549.2 35.0 %reduce-scatter.9.cloned.1.call-done = bf16[288,2304]{1,0:T(8,128)(2,1)} async-done(((bf16[2304,2304]{1,0:T(8,128)(2,1)}), bf16[288,2304]{1,0:T(8,128)(2,1)}) %reduce-scatter.9.cloned.1.call-update) | async-done | bytes 1327120 | tf_op jit(solution)/shard_map/reduce_scatter | solution.py:787
  1595.6 12.5 collective-permute-done.142.rest_3_
  1611.5 9.1 collective-permute-done.139.rest_1_
  (844 shorter events, 829.6 us)
Async XLA Ops:
  11.9 97.6 %all-gather.9.cloned.1.call-start = ((), (), s32[]{:S(2)}) async-start(), calls=%async_computation.5 | async-start | bytes 2654208 | tf_op jit(solution)/shard_map/all_gather | solution.py:783
  46.3 115.2 %all-gather.11.cloned.1.call-start = ((), (), s32[]{:S(2)}) async-start(), calls=%async_computation.6 | async-start | bytes 2654208 | tf_op jit(solution)/shard_map/all_gather | solution.py:783
  47.0 302.8 %all-gather.13.cloned.1.call-start = ((), (), s32[]{:S(2)}) async-start(), calls=%async_computation.7 | async-start | bytes 11943936 | tf_op jit(solution)/shard_map/all_gather | solution.py:783
  151.8 198.1 %all-gather.15.cloned.1.call-start = ((), (), s32[]{:S(2)}) async-start(), calls=%async_computation.8 | async-start | bytes 11943936 | tf_op jit(solution)/shard_map/all_gather | solution.py:783
  152.4 223.7 %all-gather.17.cloned.1.call-start = ((), (), s32[]{:S(2)}) async-start(), calls=%async_computation.9 | async-start | bytes 11943936 | tf_op jit(solution)/shard_map/all_gather | solution.py:783
  152.9 1179.2 %reduce-scatter.5.cloned.1.call-start = ((), (), s32[]{:S(2)}) async-start(), calls=%async_computation.10 | async-start | bytes 11943936 | tf_op jit(solution)/shard_map/reduce_scatter | solution.py:787
  234.7 63.3 %collective-permute-start.18 = (bf16[256,2304]{1,0:T(8,128)(2,1)}, bf16[256,2304]{1,0:T(8,128)(2,1)}, u32[]{:S(2)}, u32[]{:S(2)}) collective-permute-start(bf16[256,2304]{1,0:T(8,128)(2,1)} %copy-done.92), channel_id=1, source_target_pairs={{0,1},{3,2},{4,5},{7,6},{8,9},{11,10},{12,13},{15,14},{16,17},{19,... | collective-permute-start | bytes 3538952 | tf_op jit(solution)/shard_map/ppermute | solution.py:852
  254.8 68.5 %collective-permute-start.21 = (bf16[256,2304]{1,0:T(8,128)(2,1)}, bf16[256,2304]{1,0:T(8,128)(2,1)}, u32[]{:S(2)}, u32[]{:S(2)}) collective-permute-start(bf16[256,2304]{1,0:T(8,128)(2,1)} %copy-done.83), channel_id=1, source_target_pairs={{0,1},{3,2},{4,5},{7,6},{8,9},{11,10},{12,13},{15,14},{16,17},{19,... | collective-permute-start | bytes 3538952 | tf_op jit(solution)/shard_map/ppermute | solution.py:852
  310.3 76.3 %collective-permute-start.25 = (bf16[256,2304]{1,0:T(8,128)(2,1)}, bf16[256,2304]{1,0:T(8,128)(2,1)}, u32[]{:S(2)}, u32[]{:S(2)}) collective-permute-start(bf16[256,2304]{1,0:T(8,128)(2,1)} %get-tuple-element.802.refs_2_), channel_id=1, source_target_pairs={{1,2},{2,1},{5,6},{6,5},{9,10},{10,9},{13,14},{14,13},{17,18},{18,... | collective-permute-start | bytes 3538952 | tf_op jit(solution)/shard_map/ppermute | solution.py:858
  323.4 63.2 %collective-permute-start.26 = (bf16[256,2304]{1,0:T(8,128)(2,1)}, bf16[256,2304]{1,0:T(8,128)(2,1)}, u32[]{:S(2)}, u32[]{:S(2)}) collective-permute-start(bf16[256,2304]{1,0:T(8,128)(2,1)} %get-tuple-element.787.rest_0_), channel_id=1, source_target_pairs={{1,0},{2,3},{5,4},{6,7},{9,8},{10,11},{13,12},{14,15},{17,16},{18,... | collective-permute-start | bytes 3538952 | tf_op jit(solution)/shard_map/ppermute | solution.py:861
  324.7 74.5 %collective-permute-start.27 = (bf16[256,2304]{1,0:T(8,128)(2,1)S(1)}, bf16[256,2304]{1,0:T(8,128)(2,1)}, u32[]{:S(2)}, u32[]{:S(2)}) collective-permute-start(bf16[256,2304]{1,0:T(8,128)(2,1)S(1)} %get-tuple-element.808.refs_0_), channel_id=1, source_target_pairs={{0,1},{3,2},{4,5},{7,6},{8,9},{11,10},{12,13},{15,14},{16,17},{19,... | collective-permute-start | bytes 3538952 | tf_op jit(solution)/shard_map/ppermute | solution.py:852
  336.0 64.4 %collective-permute-start.28 = (bf16[256,2304]{1,0:T(8,128)(2,1)}, bf16[256,2304]{1,0:T(8,128)(2,1)}, u32[]{:S(2)}, u32[]{:S(2)}) collective-permute-start(bf16[256,2304]{1,0:T(8,128)(2,1)} %get-tuple-element.810.refs_2_), channel_id=1, source_target_pairs={{1,2},{2,1},{5,6},{6,5},{9,10},{10,9},{13,14},{14,13},{17,18},{18,... | collective-permute-start | bytes 3538952 | tf_op jit(solution)/shard_map/ppermute | solution.py:858
  348.5 58.5 %collective-permute-start.29 = (bf16[256,2304]{1,0:T(8,128)(2,1)}, bf16[256,2304]{1,0:T(8,128)(2,1)}, u32[]{:S(2)}, u32[]{:S(2)}) collective-permute-start(bf16[256,2304]{1,0:T(8,128)(2,1)} %get-tuple-element.789.rest_2_), channel_id=1, source_target_pairs={{1,0},{2,3},{5,4},{6,7},{9,8},{10,11},{13,12},{14,15},{17,16},{18,... | collective-permute-start | bytes 3538952 | tf_op jit(solution)/shard_map/ppermute | solution.py:861
  400.4 63.2 %collective-permute-start.33 = (bf16[256,2304]{1,0:T(8,128)(2,1)S(1)}, bf16[256,2304]{1,0:T(8,128)(2,1)}, u32[]{:S(2)}, u32[]{:S(2)}) collective-permute-start(bf16[256,2304]{1,0:T(8,128)(2,1)S(1)} %get-tuple-element.836.refs_0_), channel_id=1, source_target_pairs={{0,1},{3,2},{4,5},{7,6},{8,9},{11,10},{12,13},{15,14},{16,17},{19,... | collective-permute-start | bytes 3538952 | tf_op jit(solution)/shard_map/ppermute | solution.py:852
  461.9 59.1 %collective-permute-start.37 = (bf16[256,2304]{1,0:T(8,128)(2,1)}, bf16[256,2304]{1,0:T(8,128)(2,1)}, u32[]{:S(2)}, u32[]{:S(2)}) collective-permute-start(bf16[256,2304]{1,0:T(8,128)(2,1)} %get-tuple-element.858.refs_2_), channel_id=1, source_target_pairs={{1,2},{2,1},{5,6},{6,5},{9,10},{10,9},{13,14},{14,13},{17,18},{18,... | collective-permute-start | bytes 3538952 | tf_op jit(solution)/shard_map/ppermute | solution.py:858
  463.6 57.4 %collective-permute-start.38 = (bf16[256,2304]{1,0:T(8,128)(2,1)}, bf16[256,2304]{1,0:T(8,128)(2,1)}, u32[]{:S(2)}, u32[]{:S(2)}) collective-permute-start(bf16[256,2304]{1,0:T(8,128)(2,1)} %get-tuple-element.843.rest_0_), channel_id=1, source_target_pairs={{1,0},{2,3},{5,4},{6,7},{9,8},{10,11},{13,12},{14,15},{17,16},{18,... | collective-permute-start | bytes 3538952 | tf_op jit(solution)/shard_map/ppermute | solution.py:861
  464.9 68.8 %collective-permute-start.39 = (bf16[256,2304]{1,0:T(8,128)(2,1)S(1)}, bf16[256,2304]{1,0:T(8,128)(2,1)}, u32[]{:S(2)}, u32[]{:S(2)}) collective-permute-start(bf16[256,2304]{1,0:T(8,128)(2,1)S(1)} %get-tuple-element.864.refs_0_), channel_id=1, source_target_pairs={{0,1},{3,2},{4,5},{7,6},{8,9},{11,10},{12,13},{15,14},{16,17},{19,... | collective-permute-start | bytes 3538952 | tf_op jit(solution)/shard_map/ppermute | solution.py:852
  475.8 59.2 %collective-permute-start.40 = (bf16[256,2304]{1,0:T(8,128)(2,1)}, bf16[256,2304]{1,0:T(8,128)(2,1)}, u32[]{:S(2)}, u32[]{:S(2)}) collective-permute-start(bf16[256,2304]{1,0:T(8,128)(2,1)} %get-tuple-element.866.refs_2_), channel_id=1, source_target_pairs={{1,2},{2,1},{5,6},{6,5},{9,10},{10,9},{13,14},{14,13},{17,18},{18,... | collective-permute-start | bytes 3538952 | tf_op jit(solution)/shard_map/ppermute | solution.py:858
  482.9 58.8 %collective-permute-start.41 = (bf16[256,2304]{1,0:T(8,128)(2,1)}, bf16[256,2304]{1,0:T(8,128)(2,1)}, u32[]{:S(2)}, u32[]{:S(2)}) collective-permute-start(bf16[256,2304]{1,0:T(8,128)(2,1)} %get-tuple-element.845.rest_2_), channel_id=1, source_target_pairs={{1,0},{2,3},{5,4},{6,7},{9,8},{10,11},{13,12},{14,15},{17,16},{18,... | collective-permute-start | bytes 3538952 | tf_op jit(solution)/shard_map/ppermute | solution.py:861
  535.0 63.3 %collective-permute-start.45 = (bf16[256,2304]{1,0:T(8,128)(2,1)S(1)}, bf16[256,2304]{1,0:T(8,128)(2,1)}, u32[]{:S(2)}, u32[]{:S(2)}) collective-permute-start(bf16[256,2304]{1,0:T(8,128)(2,1)S(1)} %get-tuple-element.893.refs_0_), channel_id=1, source_target_pairs={{0,1},{3,2},{4,5},{7,6},{8,9},{11,10},{12,13},{15,14},{16,17},{19,... | collective-permute-start | bytes 3538952 | tf_op jit(solution)/shard_map/ppermute | solution.py:852
  547.7 58.5 %collective-permute-start.47 = (bf16[256,2304]{1,0:T(8,128)(2,1)}, bf16[256,2304]{1,0:T(8,128)(2,1)}, u32[]{:S(2)}, u32[]{:S(2)}) collective-permute-start(bf16[256,2304]{1,0:T(8,128)(2,1)} %get-tuple-element.873.rest_2_), channel_id=1, source_target_pairs={{1,0},{2,3},{5,4},{6,7},{9,8},{10,11},{13,12},{14,15},{17,16},{18,... | collective-permute-start | bytes 3538952 | tf_op jit(solution)/shard_map/ppermute | solution.py:861
  596.6 57.7 %collective-permute-start.49 = (bf16[256,2304]{1,0:T(8,128)(2,1)}, bf16[256,2304]{1,0:T(8,128)(2,1)}, u32[]{:S(2)}, u32[]{:S(2)}) collective-permute-start(bf16[256,2304]{1,0:T(8,128)(2,1)} %get-tuple-element.917.refs_2_), channel_id=1, source_target_pairs={{1,2},{2,1},{5,6},{6,5},{9,10},{10,9},{13,14},{14,13},{17,18},{18,... | collective-permute-start | bytes 3538952 | tf_op jit(solution)/shard_map/ppermute | solution.py:858
  599.6 67.4 %collective-permute-start.51 = (bf16[256,2304]{1,0:T(8,128)(2,1)S(1)}, bf16[256,2304]{1,0:T(8,128)(2,1)}, u32[]{:S(2)}, u32[]{:S(2)}) collective-permute-start(bf16[256,2304]{1,0:T(8,128)(2,1)S(1)} %get-tuple-element.923.refs_0_), channel_id=1, source_target_pairs={{0,1},{3,2},{4,5},{7,6},{8,9},{11,10},{12,13},{15,14},{16,17},{19,... | collective-permute-start | bytes 3538952 | tf_op jit(solution)/shard_map/ppermute | solution.py:852
  610.6 57.8 %collective-permute-start.52 = (bf16[256,2304]{1,0:T(8,128)(2,1)}, bf16[256,2304]{1,0:T(8,128)(2,1)}, u32[]{:S(2)}, u32[]{:S(2)}) collective-permute-start(bf16[256,2304]{1,0:T(8,128)(2,1)} %get-tuple-element.925.refs_2_), channel_id=1, source_target_pairs={{1,2},{2,1},{5,6},{6,5},{9,10},{10,9},{13,14},{14,13},{17,18},{18,... | collective-permute-start | bytes 3538952 | tf_op jit(solution)/shard_map/ppermute | solution.py:858
  612.3 62.8 %collective-permute-start.53 = (bf16[256,2304]{1,0:T(8,128)(2,1)}, bf16[256,2304]{1,0:T(8,128)(2,1)}, u32[]{:S(2)}, u32[]{:S(2)}) collective-permute-start(bf16[256,2304]{1,0:T(8,128)(2,1)} %get-tuple-element.902.rest_2_), channel_id=1, source_target_pairs={{1,0},{2,3},{5,4},{6,7},{9,8},{10,11},{13,12},{14,15},{17,16},{18,... | collective-permute-start | bytes 3538952 | tf_op jit(solution)/shard_map/ppermute | solution.py:861
  654.4 67.4 %collective-permute-start.54 = (bf16[256,2304]{1,0:T(8,128)(2,1)}, bf16[256,2304]{1,0:T(8,128)(2,1)}, u32[]{:S(2)}, u32[]{:S(2)}) collective-permute-start(bf16[256,2304]{1,0:T(8,128)(2,1)} %get-tuple-element.945.refs_0_), channel_id=1, source_target_pairs={{0,1},{3,2},{4,5},{7,6},{8,9},{11,10},{12,13},{15,14},{16,17},{19,... | collective-permute-start | bytes 3538952 | tf_op jit(solution)/shard_map/ppermute | solution.py:852
  665.4 57.6 %collective-permute-start.55 = (bf16[256,2304]{1,0:T(8,128)(2,1)}, bf16[256,2304]{1,0:T(8,128)(2,1)}, u32[]{:S(2)}, u32[]{:S(2)}) collective-permute-start(bf16[256,2304]{1,0:T(8,128)(2,1)} %get-tuple-element.947.refs_2_), channel_id=1, source_target_pairs={{1,2},{2,1},{5,6},{6,5},{9,10},{10,9},{13,14},{14,13},{17,18},{18,... | collective-permute-start | bytes 3538952 | tf_op jit(solution)/shard_map/ppermute | solution.py:858
  668.4 67.3 %collective-permute-start.57 = (bf16[256,2304]{1,0:T(8,128)(2,1)S(1)}, bf16[256,2304]{1,0:T(8,128)(2,1)}, u32[]{:S(2)}, u32[]{:S(2)}) collective-permute-start(bf16[256,2304]{1,0:T(8,128)(2,1)S(1)} %get-tuple-element.955.refs_0_), channel_id=1, source_target_pairs={{0,1},{3,2},{4,5},{7,6},{8,9},{11,10},{12,13},{15,14},{16,17},{19,... | collective-permute-start | bytes 3538952 | tf_op jit(solution)/shard_map/ppermute | solution.py:852
  679.4 57.5 %collective-permute-start.58 = (bf16[256,2304]{1,0:T(8,128)(2,1)}, bf16[256,2304]{1,0:T(8,128)(2,1)}, u32[]{:S(2)}, u32[]{:S(2)}) collective-permute-start(bf16[256,2304]{1,0:T(8,128)(2,1)} %get-tuple-element.957.refs_2_), channel_id=1, source_target_pairs={{1,2},{2,1},{5,6},{6,5},{9,10},{10,9},{13,14},{14,13},{17,18},{18,... | collective-permute-start | bytes 3538952 | tf_op jit(solution)/shard_map/ppermute | solution.py:858
  733.9 68.3 %collective-permute-start.61 = (bf16[256,2304]{1,0:T(8,128)(2,1)}, bf16[256,2304]{1,0:T(8,128)(2,1)}, u32[]{:S(2)}, u32[]{:S(2)}) collective-permute-start(bf16[256,2304]{1,0:T(8,128)(2,1)} %get-tuple-element.978.refs_2_), channel_id=1, source_target_pairs={{1,2},{2,1},{5,6},{6,5},{9,10},{10,9},{13,14},{14,13},{17,18},{18,... | collective-permute-start | bytes 3538952 | tf_op jit(solution)/shard_map/ppermute | solution.py:858
  735.6 66.6 %collective-permute-start.62 = (bf16[256,2304]{1,0:T(8,128)(2,1)}, bf16[256,2304]{1,0:T(8,128)(2,1)S(1)}, u32[]{:S(2)}, u32[]{:S(2)}) collective-permute-start(bf16[256,2304]{1,0:T(8,128)(2,1)} %get-tuple-element.951.rest_0_), channel_id=1, source_target_pairs={{1,0},{2,3},{5,4},{6,7},{9,8},{10,11},{13,12},{14,15},{17,16},{18,... | collective-permute-start | bytes 3538952 | tf_op jit(solution)/shard_map/ppermute | solution.py:861
  736.9 78.1 %collective-permute-start.63 = (bf16[256,2304]{1,0:T(8,128)(2,1)S(1)}, bf16[256,2304]{1,0:T(8,128)(2,1)}, u32[]{:S(2)}, u32[]{:S(2)}) collective-permute-start(bf16[256,2304]{1,0:T(8,128)(2,1)S(1)} %get-tuple-element.984.refs_0_), channel_id=1, source_target_pairs={{0,1},{3,2},{4,5},{7,6},{8,9},{11,10},{12,13},{15,14},{16,17},{19,... | collective-permute-start | bytes 3538952 | tf_op jit(solution)/shard_map/ppermute | solution.py:852
  757.2 59.1 %collective-permute-start.64 = (bf16[256,2304]{1,0:T(8,128)(2,1)}, bf16[256,2304]{1,0:T(8,128)(2,1)}, u32[]{:S(2)}, u32[]{:S(2)}) collective-permute-start(bf16[256,2304]{1,0:T(8,128)(2,1)} %get-tuple-element.986.refs_2_), channel_id=1, source_target_pairs={{1,2},{2,1},{5,6},{6,5},{9,10},{10,9},{13,14},{14,13},{17,18},{18,... | collective-permute-start | bytes 3538952 | tf_op jit(solution)/shard_map/ppermute | solution.py:858
  758.9 57.4 %collective-permute-start.65 = (bf16[256,2304]{1,0:T(8,128)(2,1)}, bf16[256,2304]{1,0:T(8,128)(2,1)}, u32[]{:S(2)}, u32[]{:S(2)}) collective-permute-start(bf16[256,2304]{1,0:T(8,128)(2,1)} %get-tuple-element.961.rest_2_), channel_id=1, source_target_pairs={{1,0},{2,3},{5,4},{6,7},{9,8},{10,11},{13,12},{14,15},{17,16},{18,... | collective-permute-start | bytes 3538952 | tf_op jit(solution)/shard_map/ppermute | solution.py:861
  813.3 56.7 %collective-permute-start.67 = (bf16[256,2304]{1,0:T(8,128)(2,1)}, bf16[256,2304]{1,0:T(8,128)(2,1)}, u32[]{:S(2)}, u32[]{:S(2)}) collective-permute-start(bf16[256,2304]{1,0:T(8,128)(2,1)} %get-tuple-element.1009.refs_2_), channel_id=1, source_target_pairs={{1,2},{2,1},{5,6},{6,5},{9,10},{10,9},{13,14},{14,13},{17,18},{18,... | collective-permute-start | bytes 3538952 | tf_op jit(solution)/shard_map/ppermute | solution.py:858
  816.3 66.3 %collective-permute-start.69 = (bf16[256,2304]{1,0:T(8,128)(2,1)}, bf16[256,2304]{1,0:T(8,128)(2,1)S(1)}, u32[]{:S(2)}, u32[]{:S(2)}) collective-permute-start(bf16[256,2304]{1,0:T(8,128)(2,1)} %copy-done.85), channel_id=1, source_target_pairs={{0,1},{3,2},{4,5},{7,6},{8,9},{11,10},{12,13},{15,14},{16,17},{19,... | collective-permute-start | bytes 3538952 | tf_op jit(solution)/shard_map/ppermute | solution.py:852
  825.4 59.7 %collective-permute-start.70 = (bf16[256,2304]{1,0:T(8,128)(2,1)}, bf16[256,2304]{1,0:T(8,128)(2,1)}, u32[]{:S(2)}, u32[]{:S(2)}) collective-permute-start(bf16[256,2304]{1,0:T(8,128)(2,1)} %get-tuple-element.1017.refs_2_), channel_id=1, source_target_pairs={{1,2},{2,1},{5,6},{6,5},{9,10},{10,9},{13,14},{14,13},{17,18},{18,... | collective-permute-start | bytes 3538952 | tf_op jit(solution)/shard_map/ppermute | solution.py:858
  1068.6 81.1 %collective-permute-start.87 = (bf16[512,512]{1,0:T(8,128)(2,1)}, bf16[512,512]{1,0:T(8,128)(2,1)}, u32[]{:S(2)}, u32[]{:S(2)}) collective-permute-start(bf16[512,512]{1,0:T(8,128)(2,1)} %get-tuple-element.1106), channel_id=1, source_target_pairs={{4,0},{12,8},{5,1},{13,9},{6,2},{14,10},{7,3},{15,11},{20,16},{28,... | collective-permute-start | bytes 1572872 | tf_op jit(solution)/shard_map/ppermute | solution.py:1022
  1069.9 79.8 %collective-permute-start.88 = (bf16[512,512]{1,0:T(8,128)(2,1)}, bf16[512,512]{1,0:T(8,128)(2,1)}, u32[]{:S(2)}, u32[]{:S(2)}) collective-permute-start(bf16[512,512]{1,0:T(8,128)(2,1)} %get-tuple-element.1117), channel_id=1, source_target_pairs={{8,12},{9,13},{10,14},{11,15},{24,28},{25,29},{26,30},{27,31}} | collective-permute-start | bytes 1572872 | tf_op jit(solution)/shard_map/ppermute | solution.py:1023
  1110.1 77.8 %collective-permute-start.91 = (bf16[512,512]{1,0:T(8,128)(2,1)}, bf16[512,512]{1,0:T(8,128)(2,1)}, u32[]{:S(2)}, u32[]{:S(2)}) collective-permute-start(bf16[512,512]{1,0:T(8,128)(2,1)} %pair_sums.75), channel_id=1, source_target_pairs={{8,0},{12,4},{9,1},{13,5},{10,2},{14,6},{11,3},{15,7},{24,16},{28,... | collective-permute-start | bytes 1572872 | tf_op jit(solution)/shard_map/ppermute | solution.py:1033
  1116.4 84.1 %collective-permute-start.90 = (bf16[512,512]{1,0:T(8,128)(2,1)}, bf16[512,512]{1,0:T(8,128)(2,1)}, u32[]{:S(2)}, u32[]{:S(2)}) collective-permute-start(bf16[512,512]{1,0:T(8,128)(2,1)} %pair_sums.74), channel_id=1, source_target_pairs={{8,0},{12,4},{9,1},{13,5},{10,2},{14,6},{11,3},{15,7},{24,16},{28,... | collective-permute-start | bytes 1572872 | tf_op jit(solution)/shard_map/ppermute | solution.py:1033
  1200.5 269.0 %reduce-scatter.7.cloned.1.call-start = ((), (), s32[]{:S(2)}) async-start(), calls=%async_computation.11 | async-start | bytes 11943936 | tf_op jit(solution)/shard_map/reduce_scatter | solution.py:787
  1259.0 73.1 %collective-permute-start.98 = (bf16[128,2304]{1,0:T(8,128)(2,1)}, bf16[128,2304]{1,0:T(8,128)(2,1)}, u32[]{:S(2)}, u32[]{:S(2)}) collective-permute-start(bf16[128,2304]{1,0:T(8,128)(2,1)} %get-tuple-element.1216.refs_0_), channel_id=1, source_target_pairs={{0,1},{3,2},{4,5},{7,6},{8,9},{11,10},{12,13},{15,14},{16,17},{19,... | collective-permute-start | bytes 1769480 | tf_op jit(solution)/shard_map/ppermute | solution.py:852
  1261.1 71.0 %collective-permute-start.100 = (bf16[128,2304]{1,0:T(8,128)(2,1)}, bf16[128,2304]{1,0:T(8,128)(2,1)}, u32[]{:S(2)}, u32[]{:S(2)}) collective-permute-start(bf16[128,2304]{1,0:T(8,128)(2,1)} %get-tuple-element.1225.refs_0_), channel_id=1, source_target_pairs={{0,1},{3,2},{4,5},{7,6},{8,9},{11,10},{12,13},{15,14},{16,17},{19,... | collective-permute-start | bytes 1769480 | tf_op jit(solution)/shard_map/ppermute | solution.py:852
  1332.2 251.9 %reduce-scatter.9.cloned.1.call-start = ((), (), s32[]{:S(2)}) async-start(), calls=%async_computation.12 | async-start | bytes 11943936 | tf_op jit(solution)/shard_map/reduce_scatter | solution.py:787
  1351.9 70.4 %collective-permute-start.105 = (bf16[128,2304]{1,0:T(8,128)(2,1)}, bf16[128,2304]{1,0:T(8,128)(2,1)}, u32[]{:S(2)}, u32[]{:S(2)}) collective-permute-start(bf16[128,2304]{1,0:T(8,128)(2,1)} %get-tuple-element.1241.refs_0_), channel_id=1, source_target_pairs={{0,1},{3,2},{4,5},{7,6},{8,9},{11,10},{12,13},{15,14},{16,17},{19,... | collective-permute-start | bytes 1769480 | tf_op jit(solution)/shard_map/ppermute | solution.py:852
  1354.0 77.5 %collective-permute-start.108 = (bf16[128,2304]{1,0:T(8,128)(2,1)}, bf16[128,2304]{1,0:T(8,128)(2,1)}, u32[]{:S(2)}, u32[]{:S(2)}) collective-permute-start(bf16[128,2304]{1,0:T(8,128)(2,1)} %get-tuple-element.1251.refs_0_), channel_id=1, source_target_pairs={{0,1},{3,2},{4,5},{7,6},{8,9},{11,10},{12,13},{15,14},{16,17},{19,... | collective-permute-start | bytes 1769480 | tf_op jit(solution)/shard_map/ppermute | solution.py:852
  1481.5 182.9 %reduce-scatter.11.cloned.1.call-start = ((), (), s32[]{:S(2)}) async-start(), calls=%async_computation.13 | async-start | bytes 8626176 | tf_op jit(solution)/shard_map/reduce_scatter | solution.py:787
  (311 other events, 5222.9 us)
Sparse Core Ops, SparseCore 0:
  12.0 34.1 all-gather.6
  48.1 29.0 all-gather.8
  79.1 35.0 all-gather.10
  151.9 66.1 all-gather.12
  219.8 63.7 all-gather.14
  285.4 63.7 all-gather.16
  1200.6 107.4 reduce-scatter.4
  1332.3 102.7 reduce-scatter.6
  1480.8 103.2 reduce-scatter.8
  1587.4 68.4 reduce-scatter.10

commit v2 on v1

--- a/solution.py
+++ b/solution.py
@@ -660,7 +660,7 @@
 
 def pair_sums(pairs):
     rows, columns = pairs[0][0].shape
-    tile = min(rows, ROW)
+    tile = rows // 2
     block = pl.BlockSpec((tile, columns), lambda g: (g, 0))
     return pl.pallas_call(
         pair_sums_kernel,
@@ -668,6 +668,7 @@
         grid=(rows // tile,),
         in_specs=[block] * (2 * len(pairs)),
         out_specs=[block] * len(pairs),
+        compiler_params=pltpu.CompilerParams(vmem_limit_bytes=32 * 2**20),
         cost_estimate=SMALL,
         name="pair_sums",
     )(*[array for pair in pairs for array in pair])
@@ -1061,13 +1062,12 @@
 
     def input_job(i):
         def work():
-            values[INPUT_GRAD, 0] = input_grad(
+            return {(INPUT_GRAD, i + 1): input_grad(
                 middle, values[LINEAR, i], hidden, values[MIDDLE_GRAD, i // split], i % split, gains, i,
-                values.get((INPUT_GRAD, 0)),
-            )
-            return {}
-
-        plan.job(4.0, [(LINEAR, i)], work)
+                values.get((INPUT_GRAD, i)),
+            )}
+
+        plan.job(4.0, [(LINEAR, i)] + [(INPUT_GRAD, i)] * (i > 0), work)
 
     def share_job(index, cost, needs, left, right):
         def work():
@@ -1122,8 +1122,8 @@
     share_job(GATE_SHARE, 26.0, backs, lambda: every(NORMED, count), lambda: every(GATE_LOW, count))
     share_job(UP_SHARE, 26.0, backs, lambda: every(NORMED, count), lambda: every(UP_LOW, count))
     linear_share_job()
-    scatter_job(DOWN_SHARE, 3, [(GROUP, 0)] if groups == 1 else [(BELOW, 1)])
-    scatter_job(GATE_SHARE, 3, [(TOTAL, DOWN_SHARE)])
+    scatter_job(DOWN_SHARE, 2, [(GROUP, 0)] if groups == 1 else [(BELOW, 1)])
+    scatter_job(GATE_SHARE, 2, [(TOTAL, DOWN_SHARE)])
     scatter_job(UP_SHARE, 3, [(TOTAL, GATE_SHARE)])
     scatter_job(LINEAR_SHARE, 2, [(TOTAL, UP_SHARE)])
     for i in range(fines):
@@ -1139,7 +1139,7 @@
         gain_one = gain_one + lax.ppermute(gain_one, LINE, [(i, i ^ turn) for i in range(4)])
     return (
         values[RESULT, 0][None],
-        values[INPUT_GRAD, 0][None],
+        values[INPUT_GRAD, fines][None],
         linear_share[:, :heads_width],
         linear_share[:, heads_width : heads_width + group_width],
         linear_share[:, heads_width + group_width : width],

time: 1710 us -> 1630 us (0.953)
  Pallas kernels: 835 us -> 754 us
  local copies, waits for them, and re-layouts: 114 us -> 146 us
  starting transfers between devices: 382 us -> 363 us
    pallas_call x48, Pallas kernels: 175 us -> 91 us  [pair_sums(): pl.pallas_call(pair_sums_kernel, out_shape=[jax.ShapeDtypeStruct((rows, c...]
    ppermute x40, waiting for transfers between devices: 73.8 us -> 110 us  [move(): moved[0] = (name, part, lax.ppermute(part, LINE, [(0, 1), (3, 2)]))]
    ppermute x40, waiting for transfers between devices: 91.2 us -> 57.2 us  [move(): moved[2] = (across[0], total, lax.ppermute(total, LINE, [(1, 0), (2, 3)]))]
    unnamed x411 -> x475, local copies, waits for them, and re-layouts: 102 us -> 134 us
    reduce_scatter x4, waiting for transfers between devices: 35 us -> 17 us  [scatter(): return lax.psum_scatter(grad, ROWS, scatter_dimension=0, tiled=True)]
  transfers between devices with their start and end apart: 156 -> 156, of which waited for: 29 -> 31; matrix products, arithmetic and copies ran while one was open for 2% -> 2% of each run, Pallas kernels for 47% -> 44%
where the time goes in v2:
time: 1630 us; the launch traced here: 1620 us
  Pallas kernels  754 us (46%)
  starting transfers between devices  363 us (22%)
  waiting for transfers between devices  316 us (19%)
  local copies, waits for them, and re-layouts  146 us (9%)
  other arithmetic  23.5 us (1%)
  between operations  17.9 us (1%)
    ppermute x40, starting transfers between devices, move(): moved[0] = (name, part, lax.ppermute(part, LINE, [(0, 1), (3, 2)]))  208 us
    unnamed x475, local copies, waits for them, and re-layouts  134 us
    pallas_call x6, Pallas kernels, share_call(): pl.pallas_call(functools.partial(share_kernel, number), out_shape=jax.Sha...  122 us
    pallas_call x12, Pallas kernels, back_out(): pl.pallas_call(functools.partial(back_out_kernel, number, chunk), out_sha...  111 us
    ppermute x40, waiting for transfers between devices, move(): moved[0] = (name, part, lax.ppermute(part, LINE, [(0, 1), (3, 2)]))  110 us
    pallas_call x4, Pallas kernels, gate_call(): pl.pallas_call(functools.partial(gate_kernel, number, chunk), out_shape=(...  105 us
    pallas_call x4, Pallas kernels, mixed_back(): pl.pallas_call(functools.partial(mixed_back_kernel, number, chunk), out_s...  91.4 us
    pallas_call x48, Pallas kernels, pair_sums(): pl.pallas_call(pair_sums_kernel, out_shape=[jax.ShapeDtypeStruct((rows, c...  91 us
  transfers between devices with their start and end apart: 156, of which 31 were waited for; matrix products, arithmetic and copies ran while one was open for 2% of the time, Pallas kernels for 44%

profile of v2, /device:TPU:0, one launch (start us, length us, event | category | flops | bytes accessed | tf_op | source)
XLA Modules:
  0.0 1619.1 jit_solution(159843763424190987)
XLA Ops:
  12.0 34.3 %all-gather.7.cloned.1.call-done = bf16[2304,640]{1,0:T(8,128)(2,1)} async-done(((bf16[288,640]{1,0:T(8,128)(2,1)}), bf16[2304,640]{1,0:T(8,128)(2,1)}) %all-gather.7.cloned.1.call-update) | async-done | bytes 2949136 | tf_op jit(solution)/shard_map/all_gather | solution.py:784
  57.7 11.5 project_group.1
  97.0 10.9 collective-permute-done.1.rest_1_
  206.9 14.5 collective-permute-done.13.refs_1_
  230.8 15.8 collective-permute-done.14.refs_1_
  249.4 10.6 collective-permute-start.21
  260.0 12.0 collective-permute-done.16.refs_1_
  274.4 22.8 %collective-permute-done.18.refs_1_ = bf16[256,2304]{1,0:T(8,128)(2,1)S(1)} collective-permute-done((bf16[256,2304]{1,0:T(8,128)(2,1)S(1)}, bf16[256,2304]{1,0:T(8,128)(2,1)S(1)}, u32[]{:S(2)}, u32[]{:S(2)}) %collective-permute-start.18) | collective-permute-done | bytes 1179680 | tf_op jit(solution)/shard_map/ppermute | solution.py:853
  306.3 16.1 collective-permute-done.21.refs_1_
  333.5 14.3 collective-permute-done.24.refs_1_
  350.1 26.1 %gate.4 = (bf16[512,2304]{1,0:T(8,128)(2,1)}, f32[512,2304]{1,0:T(8,128)}, bf16[512,2304]{1,0:T(8,128)(2,1)}, f32[512,2304]{1,0:T(8,128)}, f32[512,2304]{1,0:T(8,128)}, /*index=5*/bf16[512,2304]{1,0:T(8,128)(2,1)}) custom-call(s32[1]{0:T(128)} %bitcast.middle_ref, bf16[256,2304]{1,0:T(8,128)(2,1)} %copy-done.78, bf16[256,2304]{1,0:T(8,128)(2,1)} %copy-done.222, ...), custom_call_target="tpu_custom_call" | custom-call | flops 1 | bytes 1 | tf_op jit(solution)/shard_map/gate/pallas_call | solution.py:418
  378.0 9.3 back_out.16
  411.4 26.1 %gate.5 = (bf16[512,2304]{1,0:T(8,128)(2,1)}, f32[512,2304]{1,0:T(8,128)}, bf16[512,2304]{1,0:T(8,128)(2,1)}, f32[512,2304]{1,0:T(8,128)}, f32[512,2304]{1,0:T(8,128)}, /*index=5*/bf16[512,2304]{1,0:T(8,128)(2,1)}) custom-call(s32[1]{0:T(128)} %bitcast.middle_ref, bf16[256,2304]{1,0:T(8,128)(2,1)} %copy-done.76, ...), custom_call_target="tpu_custom_call" | custom-call | flops 1 | bytes 1 | tf_op jit(solution)/shard_map/gate/pallas_call | solution.py:418
  440.4 9.0 back_out.17
  472.1 8.1 collective-permute-done.36.refs_1_
  482.7 26.2 %gate.6 = (bf16[512,2304]{1,0:T(8,128)(2,1)}, f32[512,2304]{1,0:T(8,128)}, bf16[512,2304]{1,0:T(8,128)(2,1)}, f32[512,2304]{1,0:T(8,128)}, f32[512,2304]{1,0:T(8,128)}, /*index=5*/bf16[512,2304]{1,0:T(8,128)(2,1)}) custom-call(s32[1]{0:T(128)} %bitcast.middle_ref, bf16[256,2304]{1,0:T(8,128)(2,1)} %copy-done.80, ...), custom_call_target="tpu_custom_call" | custom-call | flops 1 | bytes 1 | tf_op jit(solution)/shard_map/gate/pallas_call | solution.py:418
  510.6 9.2 back_out.18
  544.7 26.2 %gate.7 = (bf16[512,2304]{1,0:T(8,128)(2,1)}, f32[512,2304]{1,0:T(8,128)}, bf16[512,2304]{1,0:T(8,128)(2,1)}, f32[512,2304]{1,0:T(8,128)}, f32[512,2304]{1,0:T(8,128)}, /*index=5*/bf16[512,2304]{1,0:T(8,128)(2,1)}) custom-call(s32[1]{0:T(128)} %bitcast.middle_ref, bf16[256,2304]{1,0:T(8,128)(2,1)} %copy-done.81, ...), custom_call_target="tpu_custom_call" | custom-call | flops 1 | bytes 1 | tf_op jit(solution)/shard_map/gate/pallas_call | solution.py:418
  572.5 9.1 back_out.19
  606.6 22.8 %mixed_back.4 = (bf16[2048,2304]{1,0:T(8,128)(2,1)}, bf16[512,2304]{1,0:T(8,128)(2,1)}, f32[8,2304]{1,0:T(8,128)}, bf16[512,2304]{1,0:T(8,128)(2,1)}, bf16[512,2304]{1,0:T(8,128)(2,1)}) custom-call(s32[1]{0:T(128)} %bitcast.middle_ref, bf16[256,2304]{1,0:T(8,128)(2,1)} %copy-done.79, bf16[256,2304]{1,0:T(8,128)(2,1)} %collective-permute-done.44.rest_1_, ...), custom_call_target="tpu_custom_call" | custom-call | flops 1 | bytes 1 | tf_op jit(solution)/shard_map/mixed_back/pallas_call | solution.py:511
  631.1 16.4 %back_out.20 = (bf16[256,2304]{1,0:T(8,128)(2,1)}, bf16[256,2304]{1,0:T(8,128)(2,1)}) custom-call(bf16[512,2304]{1,0:T(8,128)(2,1)S(1)} %copy-done.41, bf16[2304,2304]{1,0:T(8,128)(2,1)} %all-gather.13.cloned.1.call-done.rest_6_.rest_1_, bf16[512,2304]{1,0:T(8,128)(2,1)} %get-tuple-element.1177.rest_2_.rest_4_, ...), custom_call_target="tpu_custom_call" | custom-call | flops 1 | bytes 1 | tf_op jit(solution)/shard_map/back_out/pallas_call | solution.py:457
  670.4 22.8 %mixed_back.5 = (bf16[2048,2304]{1,0:T(8,128)(2,1)}, bf16[512,2304]{1,0:T(8,128)(2,1)}, f32[8,2304]{1,0:T(8,128)}, bf16[512,2304]{1,0:T(8,128)(2,1)}, bf16[512,2304]{1,0:T(8,128)(2,1)}) custom-call(s32[1]{0:T(128)} %bitcast.middle_ref, bf16[256,2304]{1,0:T(8,128)(2,1)} %copy-done.83, ...), custom_call_target="tpu_custom_call", output_to_operand_aliasing={{0}: (11, {})} | custom-call | flops 1 | bytes 1 | tf_op jit(solution)/shard_map/mixed_back/pallas_call | solution.py:511
  694.9 16.2 back_out.21
  731.3 11.7 collective-permute-done.59.rest_3_
  751.4 22.9 %mixed_back.6 = (bf16[2048,2304]{1,0:T(8,128)(2,1)}, bf16[512,2304]{1,0:T(8,128)(2,1)}, f32[8,2304]{1,0:T(8,128)}, bf16[512,2304]{1,0:T(8,128)(2,1)}, bf16[512,2304]{1,0:T(8,128)(2,1)}) custom-call(s32[1]{0:T(128)} %bitcast.middle_ref, bf16[256,2304]{1,0:T(8,128)(2,1)} %copy-done.77, ...), custom_call_target="tpu_custom_call", output_to_operand_aliasing={{0}: (11, {})} | custom-call | flops 1 | bytes 1 | tf_op jit(solution)/shard_map/mixed_back/pallas_call | solution.py:511
  776.0 16.3 %back_out.22 = (bf16[256,2304]{1,0:T(8,128)(2,1)}, bf16[256,2304]{1,0:T(8,128)(2,1)}) custom-call(bf16[512,2304]{1,0:T(8,128)(2,1)S(1)} %copy-done.43, bf16[2304,2304]{1,0:T(8,128)(2,1)} %all-gather.13.cloned.1.call-done.rest_6_.rest_1_, bf16[512,2304]{1,0:T(8,128)(2,1)} %get-tuple-element.1179.rest_2_.rest_6_, ...), custom_call_target="tpu_custom_call" | custom-call | flops 1 | bytes 1 | tf_op jit(solution)/shard_map/back_out/pallas_call | solution.py:457
  816.0 22.8 %mixed_back.7 = (bf16[2048,2304]{1,0:T(8,128)(2,1)}, bf16[512,2304]{1,0:T(8,128)(2,1)}, f32[8,2304]{1,0:T(8,128)}, bf16[512,2304]{1,0:T(8,128)(2,1)}, bf16[512,2304]{1,0:T(8,128)(2,1)}) custom-call(s32[1]{0:T(128)} %bitcast.middle_ref, bf16[256,2304]{1,0:T(8,128)(2,1)} %copy-done.82, ...), custom_call_target="tpu_custom_call", output_to_operand_aliasing={{0}: (11, {})} | custom-call | flops 1 | bytes 1 | tf_op jit(solution)/shard_map/mixed_back/pallas_call | solution.py:511
  841.8 16.1 back_out.23
  884.6 14.0 attention_low.4
  900.6 13.0 attend_back.4
  928.3 14.9 attention_low.5
  945.2 18.3 %attend_back.5 = (bf16[512,512]{1,0:T(8,128)(2,1)}, f32[6144,512]{1,0:T(8,128)}) custom-call(s32[4,2]{1,0:T(4,128)} %copy-done.193, bf16[2048,512]{1,0:T(8,128)(2,1)} %copy-done.16, bf16[512,512]{1,0:T(8,128)(2,1)} %copy-done.190, bf16[512,512]{1,0:T(8,128)(2,1)} %copy-done.72, f32[1024,128]{1,0:T(8,128)} %copy-done.183, ...), custom_call_target="tpu_custom_call" | custom-call | flops 1 | bytes 1 | tf_op jit(solution)/shard_map/attend_back/pallas_call | solution.py:217
  974.8 14.9 attention_low.6
  991.8 20.7 %attend_back.6 = (bf16[512,512]{1,0:T(8,128)(2,1)}, f32[6144,512]{1,0:T(8,128)}) custom-call(s32[4,2]{1,0:T(4,128)} %copy-done.193, bf16[2048,512]{1,0:T(8,128)(2,1)} %copy-done.16, bf16[512,512]{1,0:T(8,128)(2,1)} %copy-done.191, bf16[512,512]{1,0:T(8,128)(2,1)} %copy-done.70, f32[1024,128]{1,0:T(8,128)} %copy-done.182, ...), custom_call_target="tpu_custom_call" | custom-call | flops 1 | bytes 1 | tf_op jit(solution)/shard_map/attend_back/pallas_call | solution.py:217
  1012.5 14.5 attention_low.7
  1029.1 20.6 %attend_back.7 = (bf16[512,512]{1,0:T(8,128)(2,1)}, bf16[512,512]{1,0:T(8,128)(2,1)}, bf16[512,512]{1,0:T(8,128)(2,1)}, bf16[512,512]{1,0:T(8,128)(2,1)}, bf16[5...) custom-call(s32[4,2]{1,0:T(4,128)} %copy-done.193, ...), custom_call_target="tpu_custom_call" | custom-call | flops 1 | bytes 1 | tf_op jit(solution)/shard_map/attend_back/pallas_call | solution.py:217
  1060.2 30.5 %share.6 = bf16[2304,2304]{1,0:T(8,128)(2,1)} custom-call(bf16[512,2304]{1,0:T(8,128)(2,1)S(1)} %copy-done.74, bf16[512,2304]{1,0:T(8,128)(2,1)S(1)} %copy-done.75, bf16[512,2304]{1,0:T(8,128)(2,1)} %get-tuple-element.1102.rest_2_, bf16[512,2304]{1,0:T(8,128)(2,1)} %get-tuple-element.1103.rest_3_, bf16[512,2304]{1,0:T(8,128)(2,1)} %get-tuple-element.1104.rest_0_.rest_4_, ...), custom_call_target="tpu_custom_call" | custom-call | flops 1 | bytes 1 | tf_op jit(solution)/shard_map/share/pallas_call | solution.py:636
  1099.8 30.4 %share.7 = bf16[2304,2304]{1,0:T(8,128)(2,1)} custom-call(bf16[512,2304]{1,0:T(8,128)(2,1)S(1)} %copy-done.37, bf16[512,2304]{1,0:T(8,128)(2,1)S(1)} %copy-done.39, bf16[512,2304]{1,0:T(8,128)(2,1)} %get-tuple-element.1114.rest_2_, bf16[512,2304]{1,0:T(8,128)(2,1)} %get-tuple-element.1115.rest_3_, bf16[512,2304]{1,0:T(8,128)(2,1)} %get-tuple-element.1116.rest_0_.rest_4_, ...), custom_call_target="tpu_custom_call" | custom-call | flops 1 | bytes 1 | tf_op jit(solution)/shard_map/share/pallas_call | solution.py:636
  1130.2 42.1 %collective-permute-done.91.rest_1_ = bf16[512,512]{1,0:T(8,128)(2,1)} collective-permute-done((bf16[512,512]{1,0:T(8,128)(2,1)}, bf16[512,512]{1,0:T(8,128)(2,1)}, u32[]{:S(2)}, u32[]{:S(2)}) %collective-permute-start.91) | collective-permute-done | bytes 524320 | tf_op jit(solution)/shard_map/ppermute | solution.py:1034
  1172.3 11.2 collective-permute-done.90.rest_1_
  1219.4 14.9 collective-permute-start.96
  1265.6 17.0 %reduce-scatter.5.cloned.1.call-done = bf16[288,2304]{1,0:T(8,128)(2,1)} async-done(((bf16[2304,2304]{1,0:T(8,128)(2,1)}), bf16[288,2304]{1,0:T(8,128)(2,1)}) %reduce-scatter.5.cloned.1.call-update) | async-done | bytes 1327120 | tf_op jit(solution)/shard_map/reduce_scatter | solution.py:788
  1286.1 10.5 share.11
  1312.9 30.5 %share.8 = bf16[2304,2304]{1,0:T(8,128)(2,1)} custom-call(bf16[512,2304]{1,0:T(8,128)(2,1)S(1)} %copy-done.38, bf16[512,2304]{1,0:T(8,128)(2,1)S(1)} %copy-done.40, bf16[512,2304]{1,0:T(8,128)(2,1)} %get-tuple-element.1114.rest_2_, bf16[512,2304]{1,0:T(8,128)(2,1)} %get-tuple-element.1115.rest_3_, bf16[512,2304]{1,0:T(8,128)(2,1)} %get-tuple-element.1177.rest_2_.rest_4_, ...), custom_call_target="tpu_custom_call" | custom-call | flops 1 | bytes 1 | tf_op jit(solution)/shard_map/share/pallas_call | solution.py:636
  1351.7 10.1 share.9
  1370.5 10.0 share.10
  1385.4 14.8 collective-permute-done.104.rest_1_
  1444.0 9.1 collective-permute-start.120
  (907 shorter events, 759.1 us)
Async XLA Ops:
  11.9 97.5 %all-gather.9.cloned.1.call-start = ((), (), s32[]{:S(2)}) async-start(), calls=%async_computation.5 | async-start | bytes 2654208 | tf_op jit(solution)/shard_map/all_gather | solution.py:784
  46.3 115.1 %all-gather.11.cloned.1.call-start = ((), (), s32[]{:S(2)}) async-start(), calls=%async_computation.6 | async-start | bytes 2654208 | tf_op jit(solution)/shard_map/all_gather | solution.py:784
  47.0 303.1 %all-gather.13.cloned.1.call-start = ((), (), s32[]{:S(2)}) async-start(), calls=%async_computation.7 | async-start | bytes 11943936 | tf_op jit(solution)/shard_map/all_gather | solution.py:784
  151.7 198.4 %all-gather.15.cloned.1.call-start = ((), (), s32[]{:S(2)}) async-start(), calls=%async_computation.8 | async-start | bytes 11943936 | tf_op jit(solution)/shard_map/all_gather | solution.py:784
  152.3 224.0 %all-gather.17.cloned.1.call-start = ((), (), s32[]{:S(2)}) async-start(), calls=%async_computation.9 | async-start | bytes 11943936 | tf_op jit(solution)/shard_map/all_gather | solution.py:784
  152.9 1129.7 %reduce-scatter.5.cloned.1.call-start = ((), (), s32[]{:S(2)}) async-start(), calls=%async_computation.10 | async-start | bytes 11943936 | tf_op jit(solution)/shard_map/reduce_scatter | solution.py:788
  229.5 67.7 %collective-permute-start.18 = (bf16[256,2304]{1,0:T(8,128)(2,1)S(1)}, bf16[256,2304]{1,0:T(8,128)(2,1)S(1)}, u32[]{:S(2)}, u32[]{:S(2)}) collective-permute-start(bf16[256,2304]{1,0:T(8,128)(2,1)S(1)} %get-tuple-element.775.refs_0_), channel_id=1, source_target_pairs={{0,1},{3,2},{4,5},{7,6},{8,9},{11,10},{12,13},{15,14},{16,17},{19,... | collective-permute-start | bytes 3538952 | tf_op jit(solution)/shard_map/ppermute | solution.py:853
  248.0 55.2 %collective-permute-start.20 = (bf16[256,2304]{1,0:T(8,128)(2,1)S(1)}, bf16[256,2304]{1,0:T(8,128)(2,1)S(1)}, u32[]{:S(2)}, u32[]{:S(2)}) collective-permute-start(bf16[256,2304]{1,0:T(8,128)(2,1)S(1)} %get-tuple-element.759.rest_0_), channel_id=1, source_target_pairs={{1,0},{2,3},{5,4},{6,7},{9,8},{10,11},{13,12},{14,15},{17,16},{18,... | collective-permute-start | bytes 3538952 | tf_op jit(solution)/shard_map/ppermute | solution.py:862
  249.4 73.1 %collective-permute-start.21 = (bf16[256,2304]{1,0:T(8,128)(2,1)S(1)}, bf16[256,2304]{1,0:T(8,128)(2,1)S(1)}, u32[]{:S(2)}, u32[]{:S(2)}) collective-permute-start(bf16[256,2304]{1,0:T(8,128)(2,1)S(1)} %get-tuple-element.783.refs_0_), channel_id=1, source_target_pairs={{0,1},{3,2},{4,5},{7,6},{8,9},{11,10},{12,13},{15,14},{16,17},{19,... | collective-permute-start | bytes 3538952 | tf_op jit(solution)/shard_map/ppermute | solution.py:853
  304.7 82.6 %collective-permute-start.25 = (bf16[256,2304]{1,0:T(8,128)(2,1)}, bf16[256,2304]{1,0:T(8,128)(2,1)}, u32[]{:S(2)}, u32[]{:S(2)}) collective-permute-start(bf16[256,2304]{1,0:T(8,128)(2,1)} %get-tuple-element.805.refs_2_), channel_id=1, source_target_pairs={{1,2},{2,1},{5,6},{6,5},{9,10},{10,9},{13,14},{14,13},{17,18},{18,... | collective-permute-start | bytes 3538952 | tf_op jit(solution)/shard_map/ppermute | solution.py:859
  322.5 64.8 %collective-permute-start.26 = (bf16[256,2304]{1,0:T(8,128)(2,1)S(1)}, bf16[256,2304]{1,0:T(8,128)(2,1)}, u32[]{:S(2)}, u32[]{:S(2)}) collective-permute-start(bf16[256,2304]{1,0:T(8,128)(2,1)S(1)} %get-tuple-element.790.rest_0_), channel_id=1, source_target_pairs={{1,0},{2,3},{5,4},{6,7},{9,8},{10,11},{13,12},{14,15},{17,16},{18,... | collective-permute-start | bytes 3538952 | tf_op jit(solution)/shard_map/ppermute | solution.py:862
  323.8 74.4 %collective-permute-start.27 = (bf16[256,2304]{1,0:T(8,128)(2,1)}, bf16[256,2304]{1,0:T(8,128)(2,1)}, u32[]{:S(2)}, u32[]{:S(2)}) collective-permute-start(bf16[256,2304]{1,0:T(8,128)(2,1)} %get-tuple-element.811.refs_0_), channel_id=1, source_target_pairs={{0,1},{3,2},{4,5},{7,6},{8,9},{11,10},{12,13},{15,14},{16,17},{19,... | collective-permute-start | bytes 3538952 | tf_op jit(solution)/shard_map/ppermute | solution.py:853
  331.8 67.7 %collective-permute-start.28 = (bf16[256,2304]{1,0:T(8,128)(2,1)}, bf16[256,2304]{1,0:T(8,128)(2,1)}, u32[]{:S(2)}, u32[]{:S(2)}) collective-permute-start(bf16[256,2304]{1,0:T(8,128)(2,1)} %get-tuple-element.813.refs_2_), channel_id=1, source_target_pairs={{1,2},{2,1},{5,6},{6,5},{9,10},{10,9},{13,14},{14,13},{17,18},{18,... | collective-permute-start | bytes 3538952 | tf_op jit(solution)/shard_map/ppermute | solution.py:859
  348.8 57.3 %collective-permute-start.29 = (bf16[256,2304]{1,0:T(8,128)(2,1)S(1)}, bf16[256,2304]{1,0:T(8,128)(2,1)}, u32[]{:S(2)}, u32[]{:S(2)}) collective-permute-start(bf16[256,2304]{1,0:T(8,128)(2,1)S(1)} %get-tuple-element.792.rest_2_), channel_id=1, source_target_pairs={{1,0},{2,3},{5,4},{6,7},{9,8},{10,11},{13,12},{14,15},{17,16},{18,... | collective-permute-start | bytes 3538952 | tf_op jit(solution)/shard_map/ppermute | solution.py:862
  399.5 59.1 %collective-permute-start.33 = (bf16[256,2304]{1,0:T(8,128)(2,1)}, bf16[256,2304]{1,0:T(8,128)(2,1)}, u32[]{:S(2)}, u32[]{:S(2)}) collective-permute-start(bf16[256,2304]{1,0:T(8,128)(2,1)} %get-tuple-element.839.refs_0_), channel_id=1, source_target_pairs={{0,1},{3,2},{4,5},{7,6},{8,9},{11,10},{12,13},{15,14},{16,17},{19,... | collective-permute-start | bytes 3538952 | tf_op jit(solution)/shard_map/ppermute | solution.py:853
  456.8 63.1 %collective-permute-start.37 = (bf16[256,2304]{1,0:T(8,128)(2,1)S(1)}, bf16[256,2304]{1,0:T(8,128)(2,1)}, u32[]{:S(2)}, u32[]{:S(2)}) collective-permute-start(bf16[256,2304]{1,0:T(8,128)(2,1)S(1)} %get-tuple-element.861.refs_2_), channel_id=1, source_target_pairs={{1,2},{2,1},{5,6},{6,5},{9,10},{10,9},{13,14},{14,13},{17,18},{18,... | collective-permute-start | bytes 3538952 | tf_op jit(solution)/shard_map/ppermute | solution.py:859
  458.5 61.3 %collective-permute-start.38 = (bf16[256,2304]{1,0:T(8,128)(2,1)S(1)}, bf16[256,2304]{1,0:T(8,128)(2,1)}, u32[]{:S(2)}, u32[]{:S(2)}) collective-permute-start(bf16[256,2304]{1,0:T(8,128)(2,1)S(1)} %get-tuple-element.846.rest_0_), channel_id=1, source_target_pairs={{1,0},{2,3},{5,4},{6,7},{9,8},{10,11},{13,12},{14,15},{17,16},{18,... | collective-permute-start | bytes 3538952 | tf_op jit(solution)/shard_map/ppermute | solution.py:862
  459.8 69.2 %collective-permute-start.39 = (bf16[256,2304]{1,0:T(8,128)(2,1)}, bf16[256,2304]{1,0:T(8,128)(2,1)}, u32[]{:S(2)}, u32[]{:S(2)}) collective-permute-start(bf16[256,2304]{1,0:T(8,128)(2,1)} %get-tuple-element.867.refs_0_), channel_id=1, source_target_pairs={{0,1},{3,2},{4,5},{7,6},{8,9},{11,10},{12,13},{15,14},{16,17},{19,... | collective-permute-start | bytes 3538952 | tf_op jit(solution)/shard_map/ppermute | solution.py:853
  470.4 59.8 %collective-permute-start.40 = (bf16[256,2304]{1,0:T(8,128)(2,1)}, bf16[256,2304]{1,0:T(8,128)(2,1)}, u32[]{:S(2)}, u32[]{:S(2)}) collective-permute-start(bf16[256,2304]{1,0:T(8,128)(2,1)} %get-tuple-element.869.refs_2_), channel_id=1, source_target_pairs={{1,2},{2,1},{5,6},{6,5},{9,10},{10,9},{13,14},{14,13},{17,18},{18,... | collective-permute-start | bytes 3538952 | tf_op jit(solution)/shard_map/ppermute | solution.py:859
  481.3 55.6 %collective-permute-start.41 = (bf16[256,2304]{1,0:T(8,128)(2,1)}, bf16[256,2304]{1,0:T(8,128)(2,1)}, u32[]{:S(2)}, u32[]{:S(2)}) collective-permute-start(bf16[256,2304]{1,0:T(8,128)(2,1)} %get-tuple-element.848.rest_2_), channel_id=1, source_target_pairs={{1,0},{2,3},{5,4},{6,7},{9,8},{10,11},{13,12},{14,15},{17,16},{18,... | collective-permute-start | bytes 3538952 | tf_op jit(solution)/shard_map/ppermute | solution.py:862
  530.3 60.5 %collective-permute-start.45 = (bf16[256,2304]{1,0:T(8,128)(2,1)}, bf16[256,2304]{1,0:T(8,128)(2,1)}, u32[]{:S(2)}, u32[]{:S(2)}) collective-permute-start(bf16[256,2304]{1,0:T(8,128)(2,1)} %get-tuple-element.896.refs_0_), channel_id=1, source_target_pairs={{0,1},{3,2},{4,5},{7,6},{8,9},{11,10},{12,13},{15,14},{16,17},{19,... | collective-permute-start | bytes 3538952 | tf_op jit(solution)/shard_map/ppermute | solution.py:853
  543.4 55.3 %collective-permute-start.47 = (bf16[256,2304]{1,0:T(8,128)(2,1)}, bf16[256,2304]{1,0:T(8,128)(2,1)}, u32[]{:S(2)}, u32[]{:S(2)}) collective-permute-start(bf16[256,2304]{1,0:T(8,128)(2,1)} %get-tuple-element.876.rest_2_), channel_id=1, source_target_pairs={{1,0},{2,3},{5,4},{6,7},{9,8},{10,11},{13,12},{14,15},{17,16},{18,... | collective-permute-start | bytes 3538952 | tf_op jit(solution)/shard_map/ppermute | solution.py:862
  589.0 58.5 %collective-permute-start.49 = (bf16[256,2304]{1,0:T(8,128)(2,1)S(1)}, bf16[256,2304]{1,0:T(8,128)(2,1)}, u32[]{:S(2)}, u32[]{:S(2)}) collective-permute-start(bf16[256,2304]{1,0:T(8,128)(2,1)S(1)} %get-tuple-element.920.refs_2_), channel_id=1, source_target_pairs={{1,2},{2,1},{5,6},{6,5},{9,10},{10,9},{13,14},{14,13},{17,18},{18,... | collective-permute-start | bytes 3538952 | tf_op jit(solution)/shard_map/ppermute | solution.py:859
  590.8 56.7 %collective-permute-start.50 = (bf16[256,2304]{1,0:T(8,128)(2,1)S(1)}, bf16[256,2304]{1,0:T(8,128)(2,1)}, u32[]{:S(2)}, u32[]{:S(2)}) collective-permute-start(bf16[256,2304]{1,0:T(8,128)(2,1)S(1)} %get-tuple-element.903.rest_0_), channel_id=1, source_target_pairs={{1,0},{2,3},{5,4},{6,7},{9,8},{10,11},{13,12},{14,15},{17,16},{18,... | collective-permute-start | bytes 3538952 | tf_op jit(solution)/shard_map/ppermute | solution.py:862
  592.1 65.1 %collective-permute-start.51 = (bf16[256,2304]{1,0:T(8,128)(2,1)}, bf16[256,2304]{1,0:T(8,128)(2,1)}, u32[]{:S(2)}, u32[]{:S(2)}) collective-permute-start(bf16[256,2304]{1,0:T(8,128)(2,1)} %get-tuple-element.926.refs_0_), channel_id=1, source_target_pairs={{0,1},{3,2},{4,5},{7,6},{8,9},{11,10},{12,13},{15,14},{16,17},{19,... | collective-permute-start | bytes 3538952 | tf_op jit(solution)/shard_map/ppermute | solution.py:853
  602.3 56.2 %collective-permute-start.52 = (bf16[256,2304]{1,0:T(8,128)(2,1)}, bf16[256,2304]{1,0:T(8,128)(2,1)}, u32[]{:S(2)}, u32[]{:S(2)}) collective-permute-start(bf16[256,2304]{1,0:T(8,128)(2,1)} %get-tuple-element.928.refs_2_), channel_id=1, source_target_pairs={{1,2},{2,1},{5,6},{6,5},{9,10},{10,9},{13,14},{14,13},{17,18},{18,... | collective-permute-start | bytes 3538952 | tf_op jit(solution)/shard_map/ppermute | solution.py:859
  605.1 60.0 %collective-permute-start.53 = (bf16[256,2304]{1,0:T(8,128)(2,1)}, bf16[256,2304]{1,0:T(8,128)(2,1)}, u32[]{:S(2)}, u32[]{:S(2)}) collective-permute-start(bf16[256,2304]{1,0:T(8,128)(2,1)} %get-tuple-element.905.rest_2_), channel_id=1, source_target_pairs={{1,0},{2,3},{5,4},{6,7},{9,8},{10,11},{13,12},{14,15},{17,16},{18,... | collective-permute-start | bytes 3538952 | tf_op jit(solution)/shard_map/ppermute | solution.py:862
  647.5 63.6 %collective-permute-start.54 = (bf16[256,2304]{1,0:T(8,128)(2,1)}, bf16[256,2304]{1,0:T(8,128)(2,1)S(1)}, u32[]{:S(2)}, u32[]{:S(2)}) collective-permute-start(bf16[256,2304]{1,0:T(8,128)(2,1)} %get-tuple-element.948.refs_0_), channel_id=1, source_target_pairs={{0,1},{3,2},{4,5},{7,6},{8,9},{11,10},{12,13},{15,14},{16,17},{19,... | collective-permute-start | bytes 3538952 | tf_op jit(solution)/shard_map/ppermute | solution.py:853
  655.6 57.8 %collective-permute-start.55 = (bf16[256,2304]{1,0:T(8,128)(2,1)}, bf16[256,2304]{1,0:T(8,128)(2,1)}, u32[]{:S(2)}, u32[]{:S(2)}) collective-permute-start(bf16[256,2304]{1,0:T(8,128)(2,1)} %get-tuple-element.950.refs_2_), channel_id=1, source_target_pairs={{1,2},{2,1},{5,6},{6,5},{9,10},{10,9},{13,14},{14,13},{17,18},{18,... | collective-permute-start | bytes 3538952 | tf_op jit(solution)/shard_map/ppermute | solution.py:859
  657.3 56.2 %collective-permute-start.56 = (bf16[256,2304]{1,0:T(8,128)(2,1)S(1)}, bf16[256,2304]{1,0:T(8,128)(2,1)}, u32[]{:S(2)}, u32[]{:S(2)}) collective-permute-start(bf16[256,2304]{1,0:T(8,128)(2,1)S(1)} %get-tuple-element.933.rest_0_), channel_id=1, source_target_pairs={{1,0},{2,3},{5,4},{6,7},{9,8},{10,11},{13,12},{14,15},{17,16},{18,... | collective-permute-start | bytes 3538952 | tf_op jit(solution)/shard_map/ppermute | solution.py:862
  658.6 64.9 %collective-permute-start.57 = (bf16[256,2304]{1,0:T(8,128)(2,1)}, bf16[256,2304]{1,0:T(8,128)(2,1)}, u32[]{:S(2)}, u32[]{:S(2)}) collective-permute-start(bf16[256,2304]{1,0:T(8,128)(2,1)} %get-tuple-element.958.refs_0_), channel_id=1, source_target_pairs={{0,1},{3,2},{4,5},{7,6},{8,9},{11,10},{12,13},{15,14},{16,17},{19,... | collective-permute-start | bytes 3538952 | tf_op jit(solution)/shard_map/ppermute | solution.py:853
  668.7 56.0 %collective-permute-start.58 = (bf16[256,2304]{1,0:T(8,128)(2,1)}, bf16[256,2304]{1,0:T(8,128)(2,1)}, u32[]{:S(2)}, u32[]{:S(2)}) collective-permute-start(bf16[256,2304]{1,0:T(8,128)(2,1)} %get-tuple-element.960.refs_2_), channel_id=1, source_target_pairs={{1,2},{2,1},{5,6},{6,5},{9,10},{10,9},{13,14},{14,13},{17,18},{18,... | collective-permute-start | bytes 3538952 | tf_op jit(solution)/shard_map/ppermute | solution.py:859
  721.7 70.6 %collective-permute-start.61 = (bf16[256,2304]{1,0:T(8,128)(2,1)S(1)}, bf16[256,2304]{1,0:T(8,128)(2,1)}, u32[]{:S(2)}, u32[]{:S(2)}) collective-permute-start(bf16[256,2304]{1,0:T(8,128)(2,1)S(1)} %get-tuple-element.981.refs_2_), channel_id=1, source_target_pairs={{1,2},{2,1},{5,6},{6,5},{9,10},{10,9},{13,14},{14,13},{17,18},{18,... | collective-permute-start | bytes 3538952 | tf_op jit(solution)/shard_map/ppermute | solution.py:859
  723.5 68.9 %collective-permute-start.62 = (bf16[256,2304]{1,0:T(8,128)(2,1)S(1)}, bf16[256,2304]{1,0:T(8,128)(2,1)}, u32[]{:S(2)}, u32[]{:S(2)}) collective-permute-start(bf16[256,2304]{1,0:T(8,128)(2,1)S(1)} %get-tuple-element.954.rest_0_), channel_id=1, source_target_pairs={{1,0},{2,3},{5,4},{6,7},{9,8},{10,11},{13,12},{14,15},{17,16},{18,... | collective-permute-start | bytes 3538952 | tf_op jit(solution)/shard_map/ppermute | solution.py:862
  724.8 78.2 %collective-permute-start.63 = (bf16[256,2304]{1,0:T(8,128)(2,1)}, bf16[256,2304]{1,0:T(8,128)(2,1)}, u32[]{:S(2)}, u32[]{:S(2)}) collective-permute-start(bf16[256,2304]{1,0:T(8,128)(2,1)} %get-tuple-element.987.refs_0_), channel_id=1, source_target_pairs={{0,1},{3,2},{4,5},{7,6},{8,9},{11,10},{12,13},{15,14},{16,17},{19,... | collective-permute-start | bytes 3538952 | tf_op jit(solution)/shard_map/ppermute | solution.py:853
  747.0 57.3 %collective-permute-start.64 = (bf16[256,2304]{1,0:T(8,128)(2,1)}, bf16[256,2304]{1,0:T(8,128)(2,1)}, u32[]{:S(2)}, u32[]{:S(2)}) collective-permute-start(bf16[256,2304]{1,0:T(8,128)(2,1)} %get-tuple-element.989.refs_2_), channel_id=1, source_target_pairs={{1,2},{2,1},{5,6},{6,5},{9,10},{10,9},{13,14},{14,13},{17,18},{18,... | collective-permute-start | bytes 3538952 | tf_op jit(solution)/shard_map/ppermute | solution.py:859
  801.3 56.7 %collective-permute-start.67 = (bf16[256,2304]{1,0:T(8,128)(2,1)}, bf16[256,2304]{1,0:T(8,128)(2,1)}, u32[]{:S(2)}, u32[]{:S(2)}) collective-permute-start(bf16[256,2304]{1,0:T(8,128)(2,1)} %get-tuple-element.1012.refs_2_), channel_id=1, source_target_pairs={{1,2},{2,1},{5,6},{6,5},{9,10},{10,9},{13,14},{14,13},{17,18},{18,... | collective-permute-start | bytes 3538952 | tf_op jit(solution)/shard_map/ppermute | solution.py:859
  803.0 55.0 %collective-permute-start.68 = (bf16[256,2304]{1,0:T(8,128)(2,1)S(1)}, bf16[256,2304]{1,0:T(8,128)(2,1)S(1)}, u32[]{:S(2)}, u32[]{:S(2)}) collective-permute-start(bf16[256,2304]{1,0:T(8,128)(2,1)S(1)} %get-tuple-element.994.rest_0_), channel_id=1, source_target_pairs={{1,0},{2,3},{5,4},{6,7},{9,8},{10,11},{13,12},{14,15},{17,16},{18,... | collective-permute-start | bytes 3538952 | tf_op jit(solution)/shard_map/ppermute | solution.py:862
  804.3 65.5 %collective-permute-start.69 = (bf16[256,2304]{1,0:T(8,128)(2,1)}, bf16[256,2304]{1,0:T(8,128)(2,1)}, u32[]{:S(2)}, u32[]{:S(2)}) collective-permute-start(bf16[256,2304]{1,0:T(8,128)(2,1)} %get-tuple-element.1018.refs_0_), channel_id=1, source_target_pairs={{0,1},{3,2},{4,5},{7,6},{8,9},{11,10},{12,13},{15,14},{16,17},{19,... | collective-permute-start | bytes 3538952 | tf_op jit(solution)/shard_map/ppermute | solution.py:853
  814.4 56.8 %collective-permute-start.70 = (bf16[256,2304]{1,0:T(8,128)(2,1)}, bf16[256,2304]{1,0:T(8,128)(2,1)}, u32[]{:S(2)}, u32[]{:S(2)}) collective-permute-start(bf16[256,2304]{1,0:T(8,128)(2,1)} %get-tuple-element.1020.refs_2_), channel_id=1, source_target_pairs={{1,2},{2,1},{5,6},{6,5},{9,10},{10,9},{13,14},{14,13},{17,18},{18,... | collective-permute-start | bytes 3538952 | tf_op jit(solution)/shard_map/ppermute | solution.py:859
  1054.0 76.2 %collective-permute-start.87 = (bf16[512,512]{1,0:T(8,128)(2,1)}, bf16[512,512]{1,0:T(8,128)(2,1)}, u32[]{:S(2)}, u32[]{:S(2)}) collective-permute-start(bf16[512,512]{1,0:T(8,128)(2,1)} %get-tuple-element.1109), channel_id=1, source_target_pairs={{4,0},{12,8},{5,1},{13,9},{6,2},{14,10},{7,3},{15,11},{20,16},{28,... | collective-permute-start | bytes 1572872 | tf_op jit(solution)/shard_map/ppermute | solution.py:1023
  1055.3 74.9 %collective-permute-start.88 = (bf16[512,512]{1,0:T(8,128)(2,1)}, bf16[512,512]{1,0:T(8,128)(2,1)}, u32[]{:S(2)}, u32[]{:S(2)}) collective-permute-start(bf16[512,512]{1,0:T(8,128)(2,1)} %get-tuple-element.1120), channel_id=1, source_target_pairs={{8,12},{9,13},{10,14},{11,15},{24,28},{25,29},{26,30},{27,31}} | collective-permute-start | bytes 1572872 | tf_op jit(solution)/shard_map/ppermute | solution.py:1024
  1095.4 76.9 %collective-permute-start.91 = (bf16[512,512]{1,0:T(8,128)(2,1)}, bf16[512,512]{1,0:T(8,128)(2,1)}, u32[]{:S(2)}, u32[]{:S(2)}) collective-permute-start(bf16[512,512]{1,0:T(8,128)(2,1)} %pair_sums.75), channel_id=1, source_target_pairs={{8,0},{12,4},{9,1},{13,5},{10,2},{14,6},{11,3},{15,7},{24,16},{28,... | collective-permute-start | bytes 1572872 | tf_op jit(solution)/shard_map/ppermute | solution.py:1034
  1098.5 85.1 %collective-permute-start.90 = (bf16[512,512]{1,0:T(8,128)(2,1)}, bf16[512,512]{1,0:T(8,128)(2,1)}, u32[]{:S(2)}, u32[]{:S(2)}) collective-permute-start(bf16[512,512]{1,0:T(8,128)(2,1)} %pair_sums.74), channel_id=1, source_target_pairs={{8,0},{12,4},{9,1},{13,5},{10,2},{14,6},{11,3},{15,7},{24,16},{28,... | collective-permute-start | bytes 1572872 | tf_op jit(solution)/shard_map/ppermute | solution.py:1034
  1183.6 216.6 %reduce-scatter.7.cloned.1.call-start = ((), (), s32[]{:S(2)}) async-start(), calls=%async_computation.11 | async-start | bytes 11943936 | tf_op jit(solution)/shard_map/reduce_scatter | solution.py:788
  1282.7 200.6 %reduce-scatter.9.cloned.1.call-start = ((), (), s32[]{:S(2)}) async-start(), calls=%async_computation.12 | async-start | bytes 11943936 | tf_op jit(solution)/shard_map/reduce_scatter | solution.py:788
  1303.1 77.5 %collective-permute-start.102 = (bf16[128,2304]{1,0:T(8,128)(2,1)}, bf16[128,2304]{1,0:T(8,128)(2,1)}, u32[]{:S(2)}, u32[]{:S(2)}) collective-permute-start(bf16[128,2304]{1,0:T(8,128)(2,1)} %get-tuple-element.1242.refs_0_), channel_id=1, source_target_pairs={{0,1},{3,2},{4,5},{7,6},{8,9},{11,10},{12,13},{15,14},{16,17},{19,... | collective-permute-start | bytes 1769480 | tf_op jit(solution)/shard_map/ppermute | solution.py:853
  1400.3 164.4 %reduce-scatter.11.cloned.1.call-start = ((), (), s32[]{:S(2)}) async-start(), calls=%async_computation.13 | async-start | bytes 8626176 | tf_op jit(solution)/shard_map/reduce_scatter | solution.py:788
  (343 other events, 5593.3 us)
Sparse Core Ops, SparseCore 0:
  12.0 34.1 all-gather.6
  48.1 29.0 all-gather.8
  79.1 35.0 all-gather.10
  151.8 66.0 all-gather.12
  219.7 63.8 all-gather.14
  285.3 63.7 all-gather.16
  1183.7 98.8 reduce-scatter.4
  1286.7 82.2 reduce-scatter.6
  1400.4 80.4 reduce-scatter.8
  1489.0 67.3 reduce-scatter.10
